TPU v7x, 256 devices: a whole 4x4x8 slice. The times are simulated.
256 devices in a mesh: group: 8 (over x, core), dev: 32 (over y, z).
Axes of the slice: x: 4, y: 4, z: 8, core: 2. Of those that a mesh axis runs over, the one named last changes fastest.
Arguments:
- embeddings: bfloat16 [262144, 1024], P(('group', 'dev')), may hold values from -200 to 200
- cluster_ids: int32 [262144], P(('group', 'dev')), may hold values from 0 to 255, never falling along the last dimension, each value on 1 to 2048 neighbouring positions
Outputs:
- earlier_peak: float32 [262144], P(('group', 'dev'))
- later_peak: float32 [262144], P(('group', 'dev'))
Inputs may be any that keep to these rules, and one draw needn't show every extreme that they name: `cluster_ids`: cluster numbers never fall along the rows; each cluster holds 1 to 2048 rows, one exactly 2048.
All inputs are finite; a program needn't handle non-finite values.
Results may differ from a plain program's by a relative error of at most 0.00057.
Values may be sent and summed in bfloat16 or wider, within the bound.
No kernel may reach another device: no remote copies, remote signals or barrier semaphores. Data moves between devices by JAX's collectives and lax.ppermute only.
A program may use at most 64 MiB of HBM per device.

v0:
```python
import jax
import jax.numpy as jnp
from jax import lax
from jax.sharding import PartitionSpec as P

LOOK = 2


def passed_along(block, axis, distance):
    devices = range(lax.axis_size(axis))
    route = [(i - distance, i) for i in devices if i - distance in devices]
    return lax.ppermute(block, axis, route)


def unit_rows(values):
    wide = values.astype(jnp.float32)
    return (wide * lax.rsqrt(jnp.sum(wide * wide, axis=1, keepdims=True) + 1e-06)).astype(
        jnp.bfloat16
    )


def pair_peaks(normed, labels, other_rows, other_labels):
    scores = lax.dot_general(
        normed, other_rows, (((1,), (1,)), ((), ())), preferred_element_type=jnp.float32
    )
    matches = labels[:, None] == other_labels[None, :]
    masked = jnp.where(matches, scores, jnp.float32(-1.0))
    return (jnp.max(masked, axis=1), jnp.max(masked, axis=0))


def per_device(embeddings, cluster_ids):
    normed = unit_rows(embeddings)
    labels = cluster_ids + 1
    row_count = normed.shape[0]
    positions = jnp.arange(row_count, dtype=jnp.int32)
    shared = labels[:, None] == labels[None, :]
    own_scores = lax.dot_general(
        normed, normed, (((1,), (1,)), ((), ())), preferred_element_type=jnp.float32
    )
    earlier = jnp.max(
        jnp.where(
            shared & (positions[None, :] < positions[:, None]), own_scores, jnp.float32(-1.0)
        ),
        axis=1,
    )
    later = jnp.max(
        jnp.where(
            shared & (positions[None, :] > positions[:, None]), own_scores, jnp.float32(-1.0)
        ),
        axis=1,
    )
    offsets = list(range(1, LOOK + 1)) + [-step for step in range(1, LOOK + 1)]
    for offset in offsets:
        other_rows, other_labels = passed_along((normed, labels), ("group", "dev"), offset)
        row_peak, column_peak = pair_peaks(normed, labels, other_rows, other_labels)
        if offset > 0:
            earlier = jnp.maximum(earlier, row_peak)
        else:
            later = jnp.maximum(later, row_peak)
    return (earlier, later)


def solution(mesh):
    placed = (P(("group", "dev"), None), P(("group", "dev")))
    return jax.shard_map(
        per_device,
        mesh=mesh,
        in_specs=placed,
        out_specs=(P(("group", "dev")), P(("group", "dev"))),
        check_vma=False,
    )
```

profile of v0, /device:TPU:6, one launch (start us, length us, event | category | flops | bytes accessed | tf_op | source)
XLA Modules:
  0.0 171.6 jit_solution(14502602483751990925)
XLA Ops:
  0.6 0.0 copy-start
  0.6 2.2 %fusion = f32[1024]{0:T(1024)S(1)} fusion(bf16[1024,1024]{1,0:T(8,128)(2,1)} %param.2), kind=kLoop, calls=%fused_computation.4 | loop fusion | flops 3144704 | bytes 2101248 | tf_op jit(solution)/shard_map/reduce_sum | solution.py:17
  2.9 0.0 copy-done
  2.9 0.0 copy-start.1
  2.9 0.4 fusion.1
  3.3 10.4 %collective-permute-start.7 = (bf16[1024,1024]{1,0:T(8,128)(2,1)S(1)}, bf16[1024,1024]{1,0:T(8,128)(2,1)S(1)}, u32[]{:S(2)}, u32[]{:S(2)}) collective-permute-start(bf16[1024,1024]{1,0:T(8,128)(2,1)S(1)} %fusion.1), channel_id=1, source_target_pairs={{2,0},{3,1},{4,2},{5,3},{6,4},{7,5},{8,6},{9,7},{10,8},{11,9},{12,... | collective-permute-start | bytes 6291464 | tf_op jit(solution)/shard_map/ppermute | solution.py:12
  13.7 1.9 %collective-permute-start.3 = (bf16[1024,1024]{1,0:T(8,128)(2,1)S(1)}, bf16[1024,1024]{1,0:T(8,128)(2,1)S(1)}, u32[]{:S(2)}, u32[]{:S(2)}) collective-permute-start(bf16[1024,1024]{1,0:T(8,128)(2,1)S(1)} %fusion.1), channel_id=1, source_target_pairs={{0,2},{1,3},{2,4},{3,5},{4,6},{5,7},{6,8},{7,9},{8,10},{9,11},{10,... | collective-permute-start | bytes 6291464 | tf_op jit(solution)/shard_map/ppermute | solution.py:12
  15.6 2.9 %collective-permute-start.1 = (bf16[1024,1024]{1,0:T(8,128)(2,1)S(1)}, bf16[1024,1024]{1,0:T(8,128)(2,1)S(1)}, u32[]{:S(2)}, u32[]{:S(2)}) collective-permute-start(bf16[1024,1024]{1,0:T(8,128)(2,1)S(1)} %fusion.1), channel_id=1, source_target_pairs={{0,1},{1,2},{2,3},{3,4},{4,5},{5,6},{6,7},{7,8},{8,9},{9,10},{10,1... | collective-permute-start | bytes 6291464 | tf_op jit(solution)/shard_map/ppermute | solution.py:12
  18.5 7.3 %collective-permute-start.5 = (bf16[1024,1024]{1,0:T(8,128)(2,1)S(1)}, bf16[1024,1024]{1,0:T(8,128)(2,1)S(1)}, u32[]{:S(2)}, u32[]{:S(2)}) collective-permute-start(bf16[1024,1024]{1,0:T(8,128)(2,1)S(1)} %fusion.1), channel_id=1, source_target_pairs={{1,0},{2,1},{3,2},{4,3},{5,4},{6,5},{7,6},{8,7},{9,8},{10,9},{11,1... | collective-permute-start | bytes 6291464 | tf_op jit(solution)/shard_map/ppermute | solution.py:12
  25.9 0.0 copy-done.1
  25.9 3.4 %collective-permute-start.4 = (s32[1024]{0:T(1024)S(1)}, s32[1024]{0:T(1024)S(1)}, u32[]{:S(2)}, u32[]{:S(2)}) collective-permute-start(s32[1024]{0:T(1024)S(1)} %broadcast_add_fusion), channel_id=1, source_target_pairs={{1,0},{2,1},{3,2},{4,3},{5,4},{6,5},{7,6},{8,7},{9,8},{10,9},{11,1... | collective-permute-start | bytes 12296 | tf_op jit(solution)/shard_map/ppermute | solution.py:12
  29.2 2.4 %fusion.2 = f32[1024,1024]{0,1:T(8,128)S(1)} fusion(bf16[1024,1024]{1,0:T(8,128)(2,1)S(1)} %fusion.1), kind=kOutput, calls=%fused_computation.18 | convolution fusion | flops 2147483648 | bytes 6291456 | tf_op jit(solution)/shard_map/dot_general | solution.py:37
  31.6 73.0 %collective-permute-done.7 = bf16[1024,1024]{1,0:T(8,128)(2,1)S(1)} collective-permute-done((bf16[1024,1024]{1,0:T(8,128)(2,1)S(1)}, bf16[1024,1024]{1,0:T(8,128)(2,1)S(1)}, u32[]{:S(2)}, u32[]{:S(2)}) %collective-permute-start.7) | collective-permute-done | bytes 2097184 | tf_op jit(solution)/shard_map/ppermute | solution.py:12
  104.6 1.9 %collective-permute-start.2 = (s32[1024]{0:T(1024)S(1)}, s32[1024]{0:T(1024)S(1)}, u32[]{:S(2)}, u32[]{:S(2)}) collective-permute-start(s32[1024]{0:T(1024)S(1)} %broadcast_add_fusion), channel_id=1, source_target_pairs={{0,2},{1,3},{2,4},{3,5},{4,6},{5,7},{6,8},{7,9},{8,10},{9,11},{10,... | collective-permute-start | bytes 12296 | tf_op jit(solution)/shard_map/ppermute | solution.py:12
  106.5 2.4 %fusion.5 = f32[1024,1024]{0,1:T(8,128)S(1)} fusion(bf16[1024,1024]{1,0:T(8,128)(2,1)S(1)} %fusion.1, bf16[1024,1024]{1,0:T(8,128)(2,1)S(1)} %collective-permute-done.7), kind=kOutput, calls=%fused_computation.21 | convolution fusion | flops 2147483648 | bytes 8388608 | tf_op jit(solution)/shard_map/dot_general | solution.py:23
  108.9 3.7 %collective-permute-done.3 = bf16[1024,1024]{1,0:T(8,128)(2,1)S(1)} collective-permute-done((bf16[1024,1024]{1,0:T(8,128)(2,1)S(1)}, bf16[1024,1024]{1,0:T(8,128)(2,1)S(1)}, u32[]{:S(2)}, u32[]{:S(2)}) %collective-permute-start.3) | collective-permute-done | bytes 2097184 | tf_op jit(solution)/shard_map/ppermute | solution.py:12
  112.6 4.0 %collective-permute-start = (s32[1024]{0:T(1024)S(1)}, s32[1024]{0:T(1024)S(1)}, u32[]{:S(2)}, u32[]{:S(2)}) collective-permute-start(s32[1024]{0:T(1024)S(1)} %broadcast_add_fusion), channel_id=1, source_target_pairs={{0,1},{1,2},{2,3},{3,4},{4,5},{5,6},{6,7},{7,8},{8,9},{9,10},{10,1... | collective-permute-start | bytes 12296 | tf_op jit(solution)/shard_map/ppermute | solution.py:12
  116.5 2.4 %fusion.4 = f32[1024,1024]{0,1:T(8,128)S(1)} fusion(bf16[1024,1024]{1,0:T(8,128)(2,1)S(1)} %fusion.1, bf16[1024,1024]{1,0:T(8,128)(2,1)S(1)} %collective-permute-done.3), kind=kOutput, calls=%fused_computation.20 | convolution fusion | flops 2147483648 | bytes 8388608 | tf_op jit(solution)/shard_map/dot_general | solution.py:23
  119.0 39.2 %collective-permute-done.1 = bf16[1024,1024]{1,0:T(8,128)(2,1)S(1)} collective-permute-done((bf16[1024,1024]{1,0:T(8,128)(2,1)S(1)}, bf16[1024,1024]{1,0:T(8,128)(2,1)S(1)}, u32[]{:S(2)}, u32[]{:S(2)}) %collective-permute-start.1) | collective-permute-done | bytes 2097184 | tf_op jit(solution)/shard_map/ppermute | solution.py:12
  158.1 1.9 %collective-permute-start.6 = (s32[1024]{0:T(1024)S(1)}, s32[1024]{0:T(1024)S(1)}, u32[]{:S(2)}, u32[]{:S(2)}) collective-permute-start(s32[1024]{0:T(1024)S(1)} %broadcast_add_fusion), channel_id=1, source_target_pairs={{2,0},{3,1},{4,2},{5,3},{6,4},{7,5},{8,6},{9,7},{10,8},{11,9},{12,... | collective-permute-start | bytes 12296 | tf_op jit(solution)/shard_map/ppermute | solution.py:12
  160.1 2.4 %fusion.3 = f32[1024,1024]{0,1:T(8,128)S(1)} fusion(bf16[1024,1024]{1,0:T(8,128)(2,1)S(1)} %fusion.1, bf16[1024,1024]{1,0:T(8,128)(2,1)S(1)} %collective-permute-done.1), kind=kOutput, calls=%fused_computation.19 | convolution fusion | flops 2147483648 | bytes 8388608 | tf_op jit(solution)/shard_map/dot_general | solution.py:23
  162.5 0.0 collective-permute-done.4
  162.5 0.0 collective-permute-done.2
  162.5 0.0 collective-permute-done
  162.5 2.0 %collective-permute-done.6 = s32[1024]{0:T(1024)S(1)} collective-permute-done((s32[1024]{0:T(1024)S(1)}, s32[1024]{0:T(1024)S(1)}, u32[]{:S(2)}, u32[]{:S(2)}) %collective-permute-start.6) | collective-permute-done | bytes 4128 | tf_op jit(solution)/shard_map/ppermute | solution.py:12
  164.5 0.0 collective-permute-done.5
  164.5 6.5 %select_reduce_fusion.1 = (f32[1024]{0:T(1024)S(1)}, f32[1024]{0:T(1024)S(1)}, f32[1024]{0:T(1024)S(1)}, f32[1024]{0:T(1024)S(1)}, f32[1024]{0:T(1024)S(1)}, /*index=5*/f32[1024]{0:T(1024)S(1)}) fusion(s32[1024]{0:T(1024)S(1)} %broadcast_add_fusion, s32[1024]{0:T(1024)S(1)} %collective-permute-done.4, f32[1024,1024]{0,1:T(8,128)S(1)} %fusion.4, ...), kind=kOutput, calls=%fused_computation.7 | convolution fusion | flops 2169497600 | bytes 21016576 | tf_op jit(solution)/shard_map/dot_general | solution.py:23
  171.0 0.6 maximum_maximum_fusion
  (2 shorter events, 0.0 us)
Async XLA Ops:
  0.6 2.2 %copy-start = (bf16[1024,1024]{1,0:T(8,128)(2,1)S(1)}, bf16[1024,1024]{1,0:T(8,128)(2,1)}, u32[]{:S(2)}) copy-start(bf16[1024,1024]{1,0:T(8,128)(2,1)} %param.2) | copy-start | bytes 6291460
  2.9 23.0 %copy-start.1 = (s32[1024]{0:T(1024)S(1)}, s32[1024]{0:T(1024)}, u32[]{:S(2)}) copy-start(s32[1024]{0:T(1024)} %param.3) | copy-start | bytes 12292
  3.3 101.3 %collective-permute-start.7 = (bf16[1024,1024]{1,0:T(8,128)(2,1)S(1)}, bf16[1024,1024]{1,0:T(8,128)(2,1)S(1)}, u32[]{:S(2)}, u32[]{:S(2)}) collective-permute-start(bf16[1024,1024]{1,0:T(8,128)(2,1)S(1)} %fusion.1), channel_id=1, source_target_pairs={{2,0},{3,1},{4,2},{5,3},{6,4},{7,5},{8,6},{9,7},{10,8},{11,9},{12,... | collective-permute-start | bytes 6291464 | tf_op jit(solution)/shard_map/ppermute | solution.py:12
  13.7 98.9 %collective-permute-start.3 = (bf16[1024,1024]{1,0:T(8,128)(2,1)S(1)}, bf16[1024,1024]{1,0:T(8,128)(2,1)S(1)}, u32[]{:S(2)}, u32[]{:S(2)}) collective-permute-start(bf16[1024,1024]{1,0:T(8,128)(2,1)S(1)} %fusion.1), channel_id=1, source_target_pairs={{0,2},{1,3},{2,4},{3,5},{4,6},{5,7},{6,8},{7,9},{8,10},{9,11},{10,... | collective-permute-start | bytes 6291464 | tf_op jit(solution)/shard_map/ppermute | solution.py:12
  15.6 142.5 %collective-permute-start.1 = (bf16[1024,1024]{1,0:T(8,128)(2,1)S(1)}, bf16[1024,1024]{1,0:T(8,128)(2,1)S(1)}, u32[]{:S(2)}, u32[]{:S(2)}) collective-permute-start(bf16[1024,1024]{1,0:T(8,128)(2,1)S(1)} %fusion.1), channel_id=1, source_target_pairs={{0,1},{1,2},{2,3},{3,4},{4,5},{5,6},{6,7},{7,8},{8,9},{9,10},{10,1... | collective-permute-start | bytes 6291464 | tf_op jit(solution)/shard_map/ppermute | solution.py:12
  18.5 146.0 %collective-permute-start.5 = (bf16[1024,1024]{1,0:T(8,128)(2,1)S(1)}, bf16[1024,1024]{1,0:T(8,128)(2,1)S(1)}, u32[]{:S(2)}, u32[]{:S(2)}) collective-permute-start(bf16[1024,1024]{1,0:T(8,128)(2,1)S(1)} %fusion.1), channel_id=1, source_target_pairs={{1,0},{2,1},{3,2},{4,3},{5,4},{6,5},{7,6},{8,7},{9,8},{10,9},{11,1... | collective-permute-start | bytes 6291464 | tf_op jit(solution)/shard_map/ppermute | solution.py:12
  25.9 136.6 %collective-permute-start.4 = (s32[1024]{0:T(1024)S(1)}, s32[1024]{0:T(1024)S(1)}, u32[]{:S(2)}, u32[]{:S(2)}) collective-permute-start(s32[1024]{0:T(1024)S(1)} %broadcast_add_fusion), channel_id=1, source_target_pairs={{1,0},{2,1},{3,2},{4,3},{5,4},{6,5},{7,6},{8,7},{9,8},{10,9},{11,1... | collective-permute-start | bytes 12296 | tf_op jit(solution)/shard_map/ppermute | solution.py:12
  104.6 57.9 %collective-permute-start.2 = (s32[1024]{0:T(1024)S(1)}, s32[1024]{0:T(1024)S(1)}, u32[]{:S(2)}, u32[]{:S(2)}) collective-permute-start(s32[1024]{0:T(1024)S(1)} %broadcast_add_fusion), channel_id=1, source_target_pairs={{0,2},{1,3},{2,4},{3,5},{4,6},{5,7},{6,8},{7,9},{8,10},{9,11},{10,... | collective-permute-start | bytes 12296 | tf_op jit(solution)/shard_map/ppermute | solution.py:12
  112.6 50.0 %collective-permute-start = (s32[1024]{0:T(1024)S(1)}, s32[1024]{0:T(1024)S(1)}, u32[]{:S(2)}, u32[]{:S(2)}) collective-permute-start(s32[1024]{0:T(1024)S(1)} %broadcast_add_fusion), channel_id=1, source_target_pairs={{0,1},{1,2},{2,3},{3,4},{4,5},{5,6},{6,7},{7,8},{8,9},{9,10},{10,1... | collective-permute-start | bytes 12296 | tf_op jit(solution)/shard_map/ppermute | solution.py:12
  158.1 6.4 %collective-permute-start.6 = (s32[1024]{0:T(1024)S(1)}, s32[1024]{0:T(1024)S(1)}, u32[]{:S(2)}, u32[]{:S(2)}) collective-permute-start(s32[1024]{0:T(1024)S(1)} %broadcast_add_fusion), channel_id=1, source_target_pairs={{2,0},{3,1},{4,2},{5,3},{6,4},{7,5},{8,6},{9,7},{10,8},{11,9},{12,... | collective-permute-start | bytes 12296 | tf_op jit(solution)/shard_map/ppermute | solution.py:12
where the time goes:
time: 172 us
  waiting for transfers between devices  118 us (69%)
  starting transfers between devices  33.7 us (20%)
  matrix products  16.1 us (9%)
  other arithmetic  3.23 us (2%)
    ppermute x8, waiting for transfers between devices, passed_along(): return lax.ppermute(block, axis, route)  118 us
    ppermute x8, starting transfers between devices, passed_along(): return lax.ppermute(block, axis, route)  33.7 us
    dot_general x4, matrix products, pair_peaks(): lax.dot_general(normed, other_rows, (((1,), (1,)), ((), ())), preferred_e...  13.8 us
  transfers between devices with their start and end apart: 8, of which 4 were waited for; matrix products, arithmetic and copies ran while one was open for 6% of the time, Pallas kernels for 0%

commit v1 on v0

v1 whole, which is shorter than its diff:
```python
import functools

import jax
import jax.numpy as jnp
from jax import lax
from jax.experimental import pallas as pl
from jax.experimental.pallas import tpu as pltpu
from jax.sharding import PartitionSpec as P

ROWS = 1024
WIDTH = 1024
TILE = 256
CHUNKS = (256, 512, 256)
VMEM_LIMIT = 40 * 1024 * 1024


def passed_along(block, distance):
    axes = ("group", "dev")
    devices = range(lax.axis_size(axes))
    route = [(i - distance, i) for i in devices if i - distance in devices]
    return lax.ppermute(block, axes, route)


def unit_rows(values):
    wide = values.astype(jnp.float32)
    return (wide * lax.rsqrt(jnp.sum(wide * wide, axis=1, keepdims=True) + 1e-06)).astype(
        jnp.bfloat16
    )


def products(rows, columns):
    return lax.dot_general(
        rows, columns, (((1,), (1,)), ((), ())), preferred_element_type=jnp.float32
    )


def tail_bound(before, after):
    last = before[:, ROWS - 1 :]
    count = jnp.sum((before == after[:, :1]).astype(jnp.int32), axis=1, keepdims=True)
    return jnp.where(after == last, ROWS - count, ROWS)


def head_bound(after, before):
    first = after[:, :1]
    count = jnp.sum((after == before[:, ROWS - 1 :]).astype(jnp.int32), axis=1, keepdims=True)
    return jnp.where(before == first, count, 0)


def peak_from(rows, start, columns_ref, bound_ref, peak_ref, is_earlier):
    count = rows.shape[0]
    place = lax.broadcasted_iota(jnp.int32, (count, TILE), 0) + start

    def step(tile, carry):
        at = pl.ds(pl.multiple_of(tile * TILE, TILE), TILE)
        scores = products(rows, columns_ref[at, :])
        bound = bound_ref[:, at]
        allowed = (place >= bound) if is_earlier else (place < bound)
        best = jnp.max(jnp.where(allowed, scores, -1.0), axis=0, keepdims=True)
        peak_ref[:, at] = jnp.maximum(peak_ref[:, at], best)
        return carry

    lax.fori_loop(0, columns_ref.shape[0] // TILE, step, 0)


def own_kernel(raw_ref, row_labels_ref, column_labels_ref, normed_ref, earlier_ref, later_ref):
    def norm_step(tile, carry):
        at = pl.ds(pl.multiple_of(tile * TILE, TILE), TILE)
        normed_ref[at, :] = unit_rows(raw_ref[at, :])
        return carry

    lax.fori_loop(0, ROWS // TILE, norm_step, 0)
    earlier_ref[...] = jnp.full_like(earlier_ref, -1.0)
    later_ref[...] = jnp.full_like(later_ref, -1.0)

    def step(index, carry):
        row_tile = index // (ROWS // TILE)
        tile = index % (ROWS // TILE)
        rows_at = pl.ds(pl.multiple_of(row_tile * TILE, TILE), TILE)
        at = pl.ds(pl.multiple_of(tile * TILE, TILE), TILE)
        scores = products(normed_ref[rows_at, :], normed_ref[at, :])
        shared = row_labels_ref[rows_at, :] == column_labels_ref[:, at]
        masked = jnp.where(shared, scores, -1.0)
        place = lax.broadcasted_iota(jnp.int32, (TILE, TILE), 0) + row_tile * TILE
        other = lax.broadcasted_iota(jnp.int32, (TILE, TILE), 1) + tile * TILE
        before = jnp.max(jnp.where(place < other, masked, -1.0), axis=0, keepdims=True)
        after = jnp.max(jnp.where(place > other, masked, -1.0), axis=0, keepdims=True)
        earlier_ref[:, at] = jnp.maximum(earlier_ref[:, at], before)
        later_ref[:, at] = jnp.maximum(later_ref[:, at], after)
        return carry

    lax.fori_loop(0, (ROWS // TILE) ** 2, step, 0)


def full(shape, dtype):
    return jax.ShapeDtypeStruct(shape, dtype)


def call(kernel, outs, args, macs):
    return pl.pallas_call(
        kernel,
        out_shape=outs,
        in_specs=[pl.BlockSpec(memory_space=pltpu.VMEM)] * len(args),
        out_specs=[pl.BlockSpec(memory_space=pltpu.VMEM)] * len(outs),
        compiler_params=pltpu.CompilerParams(vmem_limit_bytes=VMEM_LIMIT),
        cost_estimate=pl.CostEstimate(
            flops=2 * macs, bytes_accessed=8 * 1024 * 1024, transcendentals=ROWS
        ),
    )(*args)


VECTOR = full((1, ROWS), jnp.float32)


def bridge_kernel(step, *refs):
    prefix = [sum(CHUNKS[:k]) for k in range(len(CHUNKS) + 1)]
    size = CHUNKS[step]
    seen = step + 1
    raw_before, raw_after = refs[:2]
    olds_before = refs[2 : 2 + step]
    olds_after = refs[2 + step : 2 + 2 * step]
    labels_before, labels_after, was_later, was_earlier = refs[2 + 2 * step : 6 + 2 * step]
    new_before, new_after, later_before, earlier_after = refs[6 + 2 * step : 10 + 2 * step]
    bound_before, bound_after = refs[10 + 2 * step :]
    new_before[...] = unit_rows(raw_before[...])
    new_after[...] = unit_rows(raw_after[...])
    later_before[...] = was_later[...]
    earlier_after[...] = was_earlier[...]
    bound_before[...] = head_bound(labels_after[...], labels_before[...])
    bound_after[...] = tail_bound(labels_before[...], labels_after[...])
    befores = list(olds_before) + [new_before]
    afters = list(olds_after) + [new_after]
    for i in range(seen):
        for j in range(seen):
            if max(i, j) != step or prefix[i] + prefix[j] + 2 > ROWS:
                continue
            low_before = ROWS - prefix[i + 1]
            low_after = prefix[j]
            peak_from(
                befores[i][...],
                low_before,
                afters[j],
                bound_after.at[:, pl.ds(low_after, CHUNKS[j])],
                earlier_after.at[:, pl.ds(low_after, CHUNKS[j])],
                True,
            )
            peak_from(
                afters[j][...],
                low_after,
                befores[i],
                bound_before.at[:, pl.ds(low_before, CHUNKS[i])],
                later_before.at[:, pl.ds(low_before, CHUNKS[i])],
                False,
            )


def side_kernel(step, before, after, normed, l_before, labels, l_after, e_in, l_in, e, l, b_e, b_l):
    prefix = sum(CHUNKS[:step])
    e[...] = e_in[...]
    l[...] = l_in[...]
    b_e[...] = tail_bound(l_before[...], labels[...])
    b_l[...] = head_bound(l_after[...], labels[...])
    peak_from(before[...], ROWS - prefix - CHUNKS[step], normed, b_e, e, True)
    peak_from(after[...], prefix, normed, b_l, l, False)


def with_scratch(kernel, outs, args, macs):
    return pl.pallas_call(
        kernel,
        out_shape=outs,
        in_specs=[pl.BlockSpec(memory_space=pltpu.VMEM)] * len(args),
        out_specs=[pl.BlockSpec(memory_space=pltpu.VMEM)] * len(outs),
        scratch_shapes=[pltpu.VMEM((1, ROWS), jnp.int32)] * 2,
        compiler_params=pltpu.CompilerParams(vmem_limit_bytes=VMEM_LIMIT),
        cost_estimate=pl.CostEstimate(
            flops=2 * macs, bytes_accessed=8 * 1024 * 1024, transcendentals=ROWS
        ),
    )(*args)


def per_device(embeddings, cluster_ids):
    steps = len(CHUNKS)
    prefix = [sum(CHUNKS[:k]) for k in range(steps + 1)]
    before, after = [], []
    source = embeddings
    for step in range(steps):
        tail = source[ROWS - prefix[step + 1] : ROWS - prefix[step]]
        head = source[prefix[step] : prefix[step + 1]]
        if step == 0:
            tail, head, source = lax.optimization_barrier((tail, head, source))
        before.append(passed_along(tail, 1))
        after.append(passed_along(head, -1))
    labels = cluster_ids + 1
    labels_before = passed_along(labels, 1).reshape(1, ROWS)
    labels_after = passed_along(labels, -1).reshape(1, ROWS)
    row = labels.reshape(1, ROWS)
    normed, earlier, later = call(
        own_kernel,
        [full((ROWS, WIDTH), jnp.bfloat16), VECTOR, VECTOR],
        (embeddings, labels.reshape(ROWS, 1), row),
        ROWS * ROWS * WIDTH,
    )
    befores, afters = [], []
    later_before = jnp.full((1, ROWS), -1.0, jnp.float32)
    earlier_after = jnp.full((1, ROWS), -1.0, jnp.float32)
    for step in range(steps):
        chunk = full((CHUNKS[step], WIDTH), jnp.bfloat16)
        new_before, new_after, later_before, earlier_after = with_scratch(
            functools.partial(bridge_kernel, step),
            [chunk, chunk, VECTOR, VECTOR],
            (
                before[step],
                after[step],
                *befores,
                *afters,
                labels_before,
                labels_after,
                later_before,
                earlier_after,
            ),
            2 * CHUNKS[step] * (ROWS - prefix[step]) * WIDTH,
        )
        befores.append(new_before)
        afters.append(new_after)
        if step == steps - 1:
            from_after = passed_along(later_before, -1)
            from_before = passed_along(earlier_after, 1)
        earlier, later = with_scratch(
            functools.partial(side_kernel, step),
            [VECTOR, VECTOR],
            (new_before, new_after, normed, labels_before, row, labels_after, earlier, later),
            2 * CHUNKS[step] * ROWS * WIDTH,
        )
    first = lax.axis_index(("group", "dev")) == 0
    last = lax.axis_index(("group", "dev")) == lax.axis_size(("group", "dev")) - 1
    earlier = jnp.maximum(earlier, jnp.where(first, -1.0, from_before))
    later = jnp.maximum(later, jnp.where(last, -1.0, from_after))
    return (earlier.reshape(ROWS), later.reshape(ROWS))


def solution(mesh):
    placed = (P(("group", "dev"), None), P(("group", "dev")))
    return jax.shard_map(
        per_device,
        mesh=mesh,
        in_specs=placed,
        out_specs=(P(("group", "dev")), P(("group", "dev"))),
        check_vma=False,
    )
```

time: 172 us -> 102 us (0.59)
  waiting for transfers between devices: 118 us -> 23.5 us
  Pallas kernels: 0 us -> 26.1 us
  matrix products: 16.1 us -> 0 us
  starting transfers between devices: 33.7 us -> 45.4 us
  local copies, waits for them, and re-layouts: 0.01 us -> 4.75 us
  other arithmetic: 3.23 us -> 1.21 us
    ppermute x8 -> x10, waiting for transfers between devices: 118 us -> 23.5 us  [passed_along(): return lax.ppermute(block, axes, route)]
    pallas_call x0 -> x7, Pallas kernels: none -> 26.1 us  [the longest x6 19.5 us: with_scratch(): pl.pallas_call(kernel, out_shape=outs, in_specs=[pl.BlockSpec(memory_spac...]
    dot_general x5 -> x0, matrix products: 16.1 us -> none  [the longest x4 13.8 us: pair_peaks(): lax.dot_general(normed, other_rows, (((1,), (1,)), ((), ())), preferred_e...]
    ppermute x8 -> x10, starting transfers between devices: 33.7 us -> 45.4 us  [passed_along(): return lax.ppermute(block, axes, route)]
    slice x0 -> x3, local copies, waits for them, and re-layouts: none -> 4.52 us  [the longest x2 3.46 us: per_device(): head = source[prefix[step]:prefix[step + 1]]]
    reduce_sum x1 -> x0, other arithmetic: 2.22 us -> none  [unit_rows(): jnp.sum(wide * wide, axis=1, keepdims=True) + 1e-06]
  transfers between devices with their start and end apart: 8 -> 10, of which waited for: 4 -> 2; matrix products, arithmetic and copies ran while one was open for 6% -> 2% of each run, Pallas kernels for 0% -> 25%
where the time goes in v1:
time: 102 us
  starting transfers between devices  45.4 us (45%)
  Pallas kernels  26.1 us (26%)
  waiting for transfers between devices  23.5 us (23%)
  local copies, waits for them, and re-layouts  4.75 us (5%)
  other arithmetic  1.21 us (1%)
    ppermute x10, starting transfers between devices, passed_along(): return lax.ppermute(block, axes, route)  45.4 us
    ppermute x10, waiting for transfers between devices, passed_along(): return lax.ppermute(block, axes, route)  23.5 us
    pallas_call x6, Pallas kernels, with_scratch(): pl.pallas_call(kernel, out_shape=outs, in_specs=[pl.BlockSpec(memory_spac...  19.5 us
    pallas_call x1, Pallas kernels, call(): pl.pallas_call(kernel, out_shape=outs, in_specs=[pl.BlockSpec(memory_spac...  6.66 us
    slice x2, local copies, waits for them, and re-layouts, per_device(): head = source[prefix[step]:prefix[step + 1]]  3.46 us
  transfers between devices with their start and end apart: 10, of which 2 were waited for; matrix products, arithmetic and copies ran while one was open for 2% of the time, Pallas kernels for 25%

profile of v1, /device:TPU:6, one launch (start us, length us, event | category | flops | bytes accessed | tf_op | source)
XLA Modules:
  0.0 101.8 jit_solution(7579150802222278778)
XLA Ops:
  0.6 0.0 copy-start
  0.6 0.0 copy-start.1
  0.6 2.4 %fusion.3 = (bf16[256,1024]{1,0:T(8,128)(2,1)}, bf16[256,1024]{1,0:T(8,128)(2,1)}) fusion(bf16[1024,1024]{1,0:T(8,128)(2,1)} %raw_ref.1), kind=kLoop, calls=%fused_computation.6 | loop fusion | bytes 2097152 | tf_op jit(solution)/shard_map/slice | solution.py:187
  3.0 0.0 copy-done
  3.0 1.1 %slice.20 = bf16[512,1024]{1,0:T(8,128)(2,1)} slice(bf16[1024,1024]{1,0:T(8,128)(2,1)S(1)} %copy-done), slice={[256:768], [0:1024]} | slice | bytes 2097152 | tf_op jit(solution)/shard_map/slice | solution.py:186
  4.1 3.8 %collective-permute-start.6 = (bf16[512,1024]{1,0:T(8,128)(2,1)}, bf16[512,1024]{1,0:T(8,128)(2,1)}, u32[]{:S(2)}, u32[]{:S(2)}) collective-permute-start(bf16[512,1024]{1,0:T(8,128)(2,1)} %slice.20), channel_id=1, source_target_pairs={{0,1},{1,2},{2,3},{3,4},{4,5},{5,6},{6,7},{7,8},{8,9},{9,10},{10,1... | collective-permute-start | bytes 3145736 | tf_op jit(solution)/shard_map/ppermute | solution.py:21
  7.9 8.0 %collective-permute-start.7 = (bf16[512,1024]{1,0:T(8,128)(2,1)}, bf16[512,1024]{1,0:T(8,128)(2,1)}, u32[]{:S(2)}, u32[]{:S(2)}) collective-permute-start(bf16[512,1024]{1,0:T(8,128)(2,1)} %slice.20), channel_id=1, source_target_pairs={{1,0},{2,1},{3,2},{4,3},{5,4},{6,5},{7,6},{8,7},{9,8},{10,9},{11,1... | collective-permute-start | bytes 3145736 | tf_op jit(solution)/shard_map/ppermute | solution.py:21
  16.0 1.9 %collective-permute-start.2 = (bf16[256,1024]{1,0:T(8,128)(2,1)}, bf16[256,1024]{1,0:T(8,128)(2,1)S(1)}, u32[]{:S(2)}, u32[]{:S(2)}) collective-permute-start(bf16[256,1024]{1,0:T(8,128)(2,1)} %get-tuple-element.27), channel_id=1, source_target_pairs={{0,1},{1,2},{2,3},{3,4},{4,5},{5,6},{6,7},{7,8},{8,9},{9,10},{10,1... | collective-permute-start | bytes 1572872 | tf_op jit(solution)/shard_map/ppermute | solution.py:21
  17.9 7.9 %collective-permute-start.3 = (bf16[256,1024]{1,0:T(8,128)(2,1)}, bf16[256,1024]{1,0:T(8,128)(2,1)}, u32[]{:S(2)}, u32[]{:S(2)}) collective-permute-start(bf16[256,1024]{1,0:T(8,128)(2,1)} %get-tuple-element.28), channel_id=1, source_target_pairs={{1,0},{2,1},{3,2},{4,3},{5,4},{6,5},{7,6},{8,7},{9,8},{10,9},{11,1... | collective-permute-start | bytes 1572872 | tf_op jit(solution)/shard_map/ppermute | solution.py:21
  25.8 0.0 copy-done.1
  25.8 1.9 %collective-permute-start.4 = (s32[1024]{0:T(1024)S(1)}, s32[1024]{0:T(1024)S(1)}, u32[]{:S(2)}, u32[]{:S(2)}) collective-permute-start(s32[1024]{0:T(1024)S(1)} %broadcast_add_fusion), channel_id=1, source_target_pairs={{0,1},{1,2},{2,3},{3,4},{4,5},{5,6},{6,7},{7,8},{8,9},{9,10},{10,1... | collective-permute-start | bytes 12296 | tf_op jit(solution)/shard_map/ppermute | solution.py:21
  27.7 21.6 %collective-permute-done.4 = s32[1024]{0:T(1024)S(1)} collective-permute-done((s32[1024]{0:T(1024)S(1)}, s32[1024]{0:T(1024)S(1)}, u32[]{:S(2)}, u32[]{:S(2)}) %collective-permute-start.4) | collective-permute-done | bytes 4128 | tf_op jit(solution)/shard_map/ppermute | solution.py:21
  49.3 2.3 %collective-permute-start.5 = (s32[1024]{0:T(1024)S(1)}, s32[1024]{0:T(1024)S(1)}, u32[]{:S(2)}, u32[]{:S(2)}) collective-permute-start(s32[1024]{0:T(1024)S(1)} %broadcast_add_fusion), channel_id=1, source_target_pairs={{1,0},{2,1},{3,2},{4,3},{5,4},{6,5},{7,6},{8,7},{9,8},{10,9},{11,1... | collective-permute-start | bytes 12296 | tf_op jit(solution)/shard_map/ppermute | solution.py:21
  51.6 1.1 %fusion.2 = (bf16[256,1024]{1,0:T(8,128)(2,1)}, bf16[256,1024]{1,0:T(8,128)(2,1)}) fusion(bf16[1024,1024]{1,0:T(8,128)(2,1)S(1)} %copy-done), kind=kLoop, calls=%fused_computation.5 | loop fusion | bytes 2097152 | tf_op jit(solution)/shard_map/slice | solution.py:187
  52.6 0.2 copy.4.row_labels_ref
  52.9 1.9 %collective-permute-done.5 = s32[1024]{0:T(1024)S(1)} collective-permute-done((s32[1024]{0:T(1024)S(1)}, s32[1024]{0:T(1024)S(1)}, u32[]{:S(2)}, u32[]{:S(2)}) %collective-permute-start.5) | collective-permute-done | bytes 4128 | tf_op jit(solution)/shard_map/ppermute | solution.py:21
  54.8 1.9 %collective-permute-start = (bf16[256,1024]{1,0:T(8,128)(2,1)}, bf16[256,1024]{1,0:T(8,128)(2,1)S(1)}, u32[]{:S(2)}, u32[]{:S(2)}) collective-permute-start(bf16[256,1024]{1,0:T(8,128)(2,1)} %get-tuple-element.51), channel_id=1, source_target_pairs={{0,1},{1,2},{2,3},{3,4},{4,5},{5,6},{6,7},{7,8},{8,9},{9,10},{10,1... | collective-permute-start | bytes 1572872 | tf_op jit(solution)/shard_map/ppermute | solution.py:21
  56.7 0.0 collective-permute-done.2.refs_0_
  56.7 7.9 %collective-permute-start.1 = (bf16[256,1024]{1,0:T(8,128)(2,1)}, bf16[256,1024]{1,0:T(8,128)(2,1)S(1)}, u32[]{:S(2)}, u32[]{:S(2)}) collective-permute-start(bf16[256,1024]{1,0:T(8,128)(2,1)} %get-tuple-element.50), channel_id=1, source_target_pairs={{1,0},{2,1},{3,2},{4,3},{5,4},{6,5},{7,6},{8,7},{9,8},{10,9},{11,1... | collective-permute-start | bytes 1572872 | tf_op jit(solution)/shard_map/ppermute | solution.py:21
  64.5 6.7 %shard_map.44 = (bf16[1024,1024]{1,0:T(8,128)(2,1)S(1)}, f32[1,1024]{1,0:T(1,128)S(1)}, f32[1,1024]{1,0:T(1,128)S(1)}) custom-call(bf16[1024,1024]{1,0:T(8,128)(2,1)S(1)} %copy-done, s32[1024,1]{1,0:T(8,128)S(1)} %copy.4.row_labels_ref, s32[1,1024]{1,0:T(1,128)S(1)} %bitcast.7), custom_call_target="tpu_custom_call" | custom-call | flops 2147483648 | bytes 8388608 | tf_op jit(solution)/shard_map/pallas_call | solution.py:99
  71.2 0.0 collective-permute-done.3.refs_1_
  71.2 1.8 %shard_map.41 = (bf16[256,1024]{1,0:T(8,128)(2,1)S(1)}, bf16[256,1024]{1,0:T(8,128)(2,1)S(1)}, f32[1,1024]{1,0:T(1,128)S(1)}, f32[1,1024]{1,0:T(1,128)S(1)}) custom-call(bf16[256,1024]{1,0:T(8,128)(2,1)S(1)} %collective-permute-done.2.refs_0_, bf16[256,1024]{1,0:T(8,128)(2,1)} %collective-permute-done.3.refs_1_, s32[1,1024]{1,0:T(1,128)S(1)} %bitcast.11, ...), custom_call_target="tpu_custom_call" | custom-call | flops 1073741824 | bytes 8388608 | tf_op jit(solution)/shard_map/pallas_call | solution.py:167
  73.1 3.0 %shard_map.45 = (f32[1,1024]{1,0:T(1,128)S(1)}, f32[1,1024]{1,0:T(1,128)S(1)}) custom-call(bf16[256,1024]{1,0:T(8,128)(2,1)S(1)} %get-tuple-element.29.refs_2_.before, bf16[256,1024]{1,0:T(8,128)(2,1)S(1)} %get-tuple-element.30.refs_3_.refs_4_.after, bf16[1024,1024]{1,0:T(8,128)(2,1)S(1)} %get-tuple-element.39.normed, s32[1,1024]{1,0:T(1,128)S(1)} %bitcast.12, ...), custom_call_target="tpu_custom_call" | custom-call | flops 1073741824 | bytes 8388608 | tf_op jit(solution)/shard_map/pallas_call | solution.py:167
  76.1 0.0 collective-permute-done.6.refs_0_
  76.1 0.0 collective-permute-done.7.refs_1_
  76.1 6.5 %shard_map.42 = (bf16[512,1024]{1,0:T(8,128)(2,1)S(1)}, bf16[512,1024]{1,0:T(8,128)(2,1)S(1)}, f32[1,1024]{1,0:T(1,128)S(1)}, f32[1,1024]{1,0:T(1,128)S(1)}) custom-call(bf16[512,1024]{1,0:T(8,128)(2,1)} %collective-permute-done.6.refs_0_, bf16[512,1024]{1,0:T(8,128)(2,1)} %collective-permute-done.7.refs_1_, ...), custom_call_target="tpu_custom_call" | custom-call | flops 1610612736 | bytes 8388608 | tf_op jit(solution)/shard_map/pallas_call | solution.py:167
  82.6 0.0 collective-permute-done.refs_0_
  82.6 0.0 collective-permute-done.1.refs_1_
  82.6 1.0 shard_map.43
  83.6 1.9 %collective-permute-start.8 = (f32[1,1024]{1,0:T(1,128)S(1)}, f32[1,1024]{1,0:T(1,128)S(1)}, u32[]{:S(2)}, u32[]{:S(2)}) collective-permute-start(f32[1,1024]{1,0:T(1,128)S(1)} %get-tuple-element.47), channel_id=1, source_target_pairs={{0,1},{1,2},{2,3},{3,4},{4,5},{5,6},{6,7},{7,8},{8,9},{9,10},{10,1... | collective-permute-start | bytes 12296 | tf_op jit(solution)/shard_map/ppermute | solution.py:21
  85.5 7.9 %collective-permute-start.9 = (f32[1,1024]{1,0:T(1,128)S(1)}, f32[1,1024]{1,0:T(1,128)S(1)}, u32[]{:S(2)}, u32[]{:S(2)}) collective-permute-start(f32[1,1024]{1,0:T(1,128)S(1)} %get-tuple-element.49), channel_id=1, source_target_pairs={{1,0},{2,1},{3,2},{4,3},{5,4},{6,5},{7,6},{8,7},{9,8},{10,9},{11,1... | collective-permute-start | bytes 12296 | tf_op jit(solution)/shard_map/ppermute | solution.py:21
  93.4 4.1 %shard_map.46 = (f32[1,1024]{1,0:T(1,128)S(1)}, f32[1,1024]{1,0:T(1,128)S(1)}) custom-call(bf16[512,1024]{1,0:T(8,128)(2,1)S(1)} %get-tuple-element.33.refs_3_.before, bf16[512,1024]{1,0:T(8,128)(2,1)S(1)} %get-tuple-element.34.refs_5_.after, bf16[1024,1024]{1,0:T(8,128)(2,1)S(1)} %get-tuple-element.39.normed, s32[1,1024]{1,0:T(1,128)S(1)} %bitcast.15, ...), custom_call_target="tpu_custom_call" | custom-call | flops 2147483648 | bytes 8388608 | tf_op jit(solution)/shard_map/pallas_call | solution.py:167
  97.6 3.0 %shard_map.47 = (f32[1,1024]{1,0:T(1,128)S(1)}, f32[1,1024]{1,0:T(1,128)S(1)}) custom-call(bf16[256,1024]{1,0:T(8,128)(2,1)S(1)} %get-tuple-element.37.before, bf16[256,1024]{1,0:T(8,128)(2,1)S(1)} %get-tuple-element.38.after, bf16[1024,1024]{1,0:T(8,128)(2,1)S(1)} %get-tuple-element.39.normed, s32[1,1024]{1,0:T(1,128)S(1)} %bitcast.16, ...), custom_call_target="tpu_custom_call" | custom-call | flops 1073741824 | bytes 8388608 | tf_op jit(solution)/shard_map/pallas_call | solution.py:167
  100.6 0.0 collective-permute-done.8
  100.6 0.6 fusion
  101.2 0.0 collective-permute-done.9
  101.2 0.6 fusion.1
  (2 shorter events, 0.0 us)
Async XLA Ops:
  0.6 2.4 %copy-start = (bf16[1024,1024]{1,0:T(8,128)(2,1)S(1)}, bf16[1024,1024]{1,0:T(8,128)(2,1)}, u32[]{:S(2)}) copy-start(bf16[1024,1024]{1,0:T(8,128)(2,1)} %raw_ref.1) | copy-start | bytes 6291460
  0.6 25.1 %copy-start.1 = (s32[1024]{0:T(1024)S(1)}, s32[1024]{0:T(1024)}, u32[]{:S(2)}) copy-start(s32[1024]{0:T(1024)} %param.3) | copy-start | bytes 12292
  4.1 72.0 %collective-permute-start.6 = (bf16[512,1024]{1,0:T(8,128)(2,1)}, bf16[512,1024]{1,0:T(8,128)(2,1)}, u32[]{:S(2)}, u32[]{:S(2)}) collective-permute-start(bf16[512,1024]{1,0:T(8,128)(2,1)} %slice.20), channel_id=1, source_target_pairs={{0,1},{1,2},{2,3},{3,4},{4,5},{5,6},{6,7},{7,8},{8,9},{9,10},{10,1... | collective-permute-start | bytes 3145736 | tf_op jit(solution)/shard_map/ppermute | solution.py:21
  7.9 68.2 %collective-permute-start.7 = (bf16[512,1024]{1,0:T(8,128)(2,1)}, bf16[512,1024]{1,0:T(8,128)(2,1)}, u32[]{:S(2)}, u32[]{:S(2)}) collective-permute-start(bf16[512,1024]{1,0:T(8,128)(2,1)} %slice.20), channel_id=1, source_target_pairs={{1,0},{2,1},{3,2},{4,3},{5,4},{6,5},{7,6},{8,7},{9,8},{10,9},{11,1... | collective-permute-start | bytes 3145736 | tf_op jit(solution)/shard_map/ppermute | solution.py:21
  16.0 40.7 %collective-permute-start.2 = (bf16[256,1024]{1,0:T(8,128)(2,1)}, bf16[256,1024]{1,0:T(8,128)(2,1)S(1)}, u32[]{:S(2)}, u32[]{:S(2)}) collective-permute-start(bf16[256,1024]{1,0:T(8,128)(2,1)} %get-tuple-element.27), channel_id=1, source_target_pairs={{0,1},{1,2},{2,3},{3,4},{4,5},{5,6},{6,7},{7,8},{8,9},{9,10},{10,1... | collective-permute-start | bytes 1572872 | tf_op jit(solution)/shard_map/ppermute | solution.py:21
  17.9 53.3 %collective-permute-start.3 = (bf16[256,1024]{1,0:T(8,128)(2,1)}, bf16[256,1024]{1,0:T(8,128)(2,1)}, u32[]{:S(2)}, u32[]{:S(2)}) collective-permute-start(bf16[256,1024]{1,0:T(8,128)(2,1)} %get-tuple-element.28), channel_id=1, source_target_pairs={{1,0},{2,1},{3,2},{4,3},{5,4},{6,5},{7,6},{8,7},{9,8},{10,9},{11,1... | collective-permute-start | bytes 1572872 | tf_op jit(solution)/shard_map/ppermute | solution.py:21
  25.8 23.5 %collective-permute-start.4 = (s32[1024]{0:T(1024)S(1)}, s32[1024]{0:T(1024)S(1)}, u32[]{:S(2)}, u32[]{:S(2)}) collective-permute-start(s32[1024]{0:T(1024)S(1)} %broadcast_add_fusion), channel_id=1, source_target_pairs={{0,1},{1,2},{2,3},{3,4},{4,5},{5,6},{6,7},{7,8},{8,9},{9,10},{10,1... | collective-permute-start | bytes 12296 | tf_op jit(solution)/shard_map/ppermute | solution.py:21
  49.3 5.5 %collective-permute-start.5 = (s32[1024]{0:T(1024)S(1)}, s32[1024]{0:T(1024)S(1)}, u32[]{:S(2)}, u32[]{:S(2)}) collective-permute-start(s32[1024]{0:T(1024)S(1)} %broadcast_add_fusion), channel_id=1, source_target_pairs={{1,0},{2,1},{3,2},{4,3},{5,4},{6,5},{7,6},{8,7},{9,8},{10,9},{11,1... | collective-permute-start | bytes 12296 | tf_op jit(solution)/shard_map/ppermute | solution.py:21
  54.8 27.8 %collective-permute-start = (bf16[256,1024]{1,0:T(8,128)(2,1)}, bf16[256,1024]{1,0:T(8,128)(2,1)S(1)}, u32[]{:S(2)}, u32[]{:S(2)}) collective-permute-start(bf16[256,1024]{1,0:T(8,128)(2,1)} %get-tuple-element.51), channel_id=1, source_target_pairs={{0,1},{1,2},{2,3},{3,4},{4,5},{5,6},{6,7},{7,8},{8,9},{9,10},{10,1... | collective-permute-start | bytes 1572872 | tf_op jit(solution)/shard_map/ppermute | solution.py:21
  56.7 25.9 %collective-permute-start.1 = (bf16[256,1024]{1,0:T(8,128)(2,1)}, bf16[256,1024]{1,0:T(8,128)(2,1)S(1)}, u32[]{:S(2)}, u32[]{:S(2)}) collective-permute-start(bf16[256,1024]{1,0:T(8,128)(2,1)} %get-tuple-element.50), channel_id=1, source_target_pairs={{1,0},{2,1},{3,2},{4,3},{5,4},{6,5},{7,6},{8,7},{9,8},{10,9},{11,1... | collective-permute-start | bytes 1572872 | tf_op jit(solution)/shard_map/ppermute | solution.py:21
  83.6 17.0 %collective-permute-start.8 = (f32[1,1024]{1,0:T(1,128)S(1)}, f32[1,1024]{1,0:T(1,128)S(1)}, u32[]{:S(2)}, u32[]{:S(2)}) collective-permute-start(f32[1,1024]{1,0:T(1,128)S(1)} %get-tuple-element.47), channel_id=1, source_target_pairs={{0,1},{1,2},{2,3},{3,4},{4,5},{5,6},{6,7},{7,8},{8,9},{9,10},{10,1... | collective-permute-start | bytes 12296 | tf_op jit(solution)/shard_map/ppermute | solution.py:21
  85.5 15.6 %collective-permute-start.9 = (f32[1,1024]{1,0:T(1,128)S(1)}, f32[1,1024]{1,0:T(1,128)S(1)}, u32[]{:S(2)}, u32[]{:S(2)}) collective-permute-start(f32[1,1024]{1,0:T(1,128)S(1)} %get-tuple-element.49), channel_id=1, source_target_pairs={{1,0},{2,1},{3,2},{4,3},{5,4},{6,5},{7,6},{8,7},{9,8},{10,9},{11,1... | collective-permute-start | bytes 12296 | tf_op jit(solution)/shard_map/ppermute | solution.py:21

commit v2 on v0

v2 whole, which is shorter than its diff:
```python
import functools

import jax
import jax.numpy as jnp
from jax import lax
from jax.experimental import pallas as pl
from jax.experimental.pallas import tpu as pltpu
from jax.sharding import PartitionSpec as P

ROWS = 1024
WIDTH = 1024
TILE = 256
CHUNKS = ((0, 256), (768, 256), (256, 384), (640, 128))
NOTE = 16
RADIX = 32
VMEM_LIMIT = 16 * 1024 * 1024
AXES = ("group", "dev")


def exchanged(block, side):
    devices = lax.axis_size(AXES)
    pairs = [(i, i + 1) for i in range(side, devices - 1, 2)]
    return lax.ppermute(block, AXES, pairs + [(b, a) for a, b in pairs])


def both_sides(block):
    return [exchanged(block, side) for side in range(2)]


def by_role(side_0, side_1):
    odd = lax.axis_index("dev") % 2 == 1
    return jnp.where(odd, side_0, side_1), jnp.where(odd, side_1, side_0)


def unit_rows(values):
    wide = values.astype(jnp.float32)
    return (wide * lax.rsqrt(jnp.sum(wide * wide, axis=1, keepdims=True) + 1e-06)).astype(
        jnp.bfloat16
    )


def products(rows, columns):
    return lax.dot_general(
        rows, columns, (((1,), (1,)), ((), ())), preferred_element_type=jnp.float32
    )


def places(shape, axis):
    return lax.broadcasted_iota(jnp.int32, shape, axis)


def best_allowed(allowed, scores):
    return jnp.max(jnp.where(allowed, scores, -1.0), axis=0, keepdims=True)


def raise_peak(peaks_ref, row, at, best):
    row = slice(row, row + 1)
    peaks_ref[row, at] = jnp.maximum(peaks_ref[row, at], best)


def edge_run(ids, edge):
    label = ids[:, edge : edge + 1]
    return label, jnp.sum((ids == label).astype(jnp.int32), axis=1, keepdims=True)


def written_note(ids):
    row = places((NOTE, WIDTH), 0)
    note = jnp.zeros((NOTE, WIDTH), jnp.int32)
    for k, edge in enumerate((0, ROWS - 1)):
        label, count = edge_run(ids, edge)
        for n, value in enumerate((label, count // RADIX, count % RADIX)):
            note = jnp.where(row == 3 * k + n, value, note)
    return note.astype(jnp.float32).astype(jnp.bfloat16)


def read_note(note, k):
    note = note.astype(jnp.float32).astype(jnp.int32)
    label, high, low = (note[3 * k + n : 3 * k + n + 1, 0:1] for n in range(3))
    return label, high * RADIX + low


def noted_kernel(raw_hbm, _, ids_ref, piece_ref, sem):
    start, size = CHUNKS[1]
    copy = pltpu.make_async_copy(
        raw_hbm.at[pl.ds(start, size)], piece_ref.at[pl.ds(0, size)], sem
    )
    copy.start()
    piece_ref[size:, :] = written_note(ids_ref[...])
    copy.wait()


def own_kernel(
    _, __, raw_ref, row_ids_ref, ids_ref, normed_ref, earlier_ref, later_ref, piece_ref
):
    start, size = CHUNKS[2]
    piece_ref[...] = raw_ref[start : start + size, :]
    for part in range(0, ROWS, 128):
        normed_ref[part : part + 128, :] = unit_rows(raw_ref[part : part + 128, :])
    earlier_ref[...] = jnp.full_like(earlier_ref, -1.0)
    later_ref[...] = jnp.full_like(later_ref, -1.0)
    tiles = ROWS // TILE
    for row_tile in range(tiles):
        rows_at = pl.ds(row_tile * TILE, TILE)
        rows = normed_ref[rows_at, :]
        for tile in range(tiles):
            at = pl.ds(tile * TILE, TILE)
            scores = products(rows, normed_ref[at, :])
            shared = row_ids_ref[rows_at, :] == ids_ref[:, at]
            row, column = places(shared.shape, 0), places(shared.shape, 1)
            if row_tile <= tile:
                allowed = shared & (row < column) if row_tile == tile else shared
                raise_peak(earlier_ref, 0, at, best_allowed(allowed, scores))
            if row_tile >= tile:
                allowed = shared & (row > column) if row_tile == tile else shared
                raise_peak(later_ref, 0, at, best_allowed(allowed, scores))


OWN_BEFORE, OWN_AFTER, AFTER_BEFORE, BEFORE_AFTER, HAS_BEFORE, HAS_AFTER = range(6)


def find_bounds(ids, note_before, note_after, bounds):
    (label_before, count_before) = read_note(note_before, 1)
    (label_after, count_after) = read_note(note_after, 0)
    first_before = ROWS - count_before
    joined = label_before == label_after
    place = places((1, ROWS), 1)
    rows = {
        OWN_BEFORE: jnp.where(ids == label_before, first_before, ROWS),
        OWN_AFTER: jnp.where(ids == label_after, count_after, 0),
        AFTER_BEFORE: jnp.where(joined & (place < count_after), first_before, ROWS),
        BEFORE_AFTER: jnp.where(joined & (place >= first_before), count_after, 0),
        HAS_BEFORE: jnp.broadcast_to(count_before, (1, ROWS)),
        HAS_AFTER: jnp.broadcast_to(count_after, (1, ROWS)),
    }
    for row, value in rows.items():
        bounds[row : row + 1, :] = value


def against_own(chunk, before, after, normed_ref, bounds, peaks):
    start, size = CHUNKS[chunk]
    place = places((size, TILE), 0) + start
    rows = jnp.concatenate([before[...], after[...]], axis=0) if size < TILE else None
    for tile in range(ROWS // TILE):
        at = pl.ds(tile * TILE, TILE)
        columns = normed_ref[at, :]
        if rows is None:
            scores = products(before[...], columns), products(after[...], columns)
        else:
            scores = products(rows, columns)
            scores = scores[:size], scores[size:]
        allowed = place >= bounds[OWN_BEFORE : OWN_BEFORE + 1, at]
        raise_peak(peaks, 0, at, best_allowed(allowed, scores[0]))
        allowed = place < bounds[OWN_AFTER : OWN_AFTER + 1, at]
        raise_peak(peaks, 1, at, best_allowed(allowed, scores[1]))


def across(chunk, befores, afters, bounds, returned):
    for i in range(chunk + 1):
        for j in range(chunk + 1):
            (low_i, size_i), (low_j, size_j) = CHUNKS[i], CHUNKS[j]
            skip_i = max(0, low_j - low_i)
            size_j = min(size_j, low_i + size_i - low_j)
            if max(i, j) != chunk or skip_i >= size_i or size_j <= 0:
                continue
            low_i, size_i = low_i + skip_i, size_i - skip_i
            rows_i = befores[i].at[pl.ds(skip_i, size_i)]
            rows_j = afters[j].at[pl.ds(0, size_j)]
            for part in range(0, size_j, TILE):
                size = min(TILE, size_j - part)
                at = pl.ds(low_j + part, size)
                scores = products(rows_i[...], rows_j[part : part + size, :])
                bound = bounds[AFTER_BEFORE : AFTER_BEFORE + 1, at]
                allowed = places(scores.shape, 0) + low_i >= bound
                raise_peak(returned, 1, at, best_allowed(allowed, scores))
            for part in range(0, size_i, TILE):
                size = min(TILE, size_i - part)
                at = pl.ds(low_i + part, size)
                scores = products(rows_j[...], rows_i[part : part + size, :])
                bound = bounds[BEFORE_AFTER : BEFORE_AFTER + 1, at]
                allowed = places(scores.shape, 0) + low_j < bound
                raise_peak(returned, 0, at, best_allowed(allowed, scores))


def take_chunk(side_0, side_1, before, after):
    for part in range(0, before.shape[0], 128):
        at = slice(part, part + 128)
        before[at, :], after[at, :] = by_role(unit_rows(side_0[at, :]), unit_rows(side_1[at, :]))


def first_kernel(raw_ref, *refs):
    got, (normed, ids_ref, _) = (refs[0:2], refs[2:4]), refs[4:7]
    befores, afters = refs[7:9], refs[9:11]
    bounds, peaks, returned, piece_ref = refs[11:]
    start, size = CHUNKS[3]
    piece_ref[...] = raw_ref[start : start + size, :]
    peaks[...] = jnp.full_like(peaks, -1.0)
    returned[...] = jnp.full_like(returned, -1.0)
    notes = by_role(*(side[CHUNKS[1][1] :, :128].astype(jnp.float32) for side in got[1]))
    find_bounds(ids_ref[...], *notes, bounds)
    for chunk in range(2):
        take_chunk(*got[chunk], befores[chunk], afters[chunk])
        against_own(chunk, befores[chunk], afters[chunk], normed, bounds, peaks)
        across(chunk, befores, afters, bounds, returned)


def next_kernel(chunk, side_0, side_1, normed, bounds, peaks_in, returned_in, *refs):
    befores, afters = refs[:chunk], refs[chunk : 2 * chunk]
    before, after, peaks, returned = refs[2 * chunk :]
    peaks[...] = peaks_in[...]
    returned[...] = returned_in[...]
    take_chunk(side_0, side_1, before, after)
    against_own(chunk, before, after, normed, bounds, peaks)
    across(chunk, [*befores, before], [*afters, after], bounds, returned)


def last_across_kernel(chunk, side_0, side_1, bounds, returned_in, *refs):
    befores, afters = refs[:chunk], refs[chunk : 2 * chunk]
    before, after, returned = refs[2 * chunk :]
    returned[...] = returned_in[...]
    take_chunk(side_0, side_1, before, after)
    across(chunk, [*befores, before], [*afters, after], bounds, returned)


def last_own_kernel(chunk, before, after, normed, bounds, peaks_in, peaks):
    peaks[...] = peaks_in[...]
    against_own(chunk, before, after, normed, bounds, peaks)


def join_kernel(earlier_in, later_in, peaks, bounds, side_0, side_1, earlier, later):
    from_before, from_after = by_role(side_0[...], side_1[...])
    has_before = bounds[HAS_BEFORE : HAS_BEFORE + 1, :] > 0
    has_after = bounds[HAS_AFTER : HAS_AFTER + 1, :] > 0
    from_before = jnp.where(has_before, from_before[1:2], -1.0)
    from_after = jnp.where(has_after, from_after[0:1], -1.0)
    earlier[...] = jnp.maximum(jnp.maximum(earlier_in[...], peaks[0:1, :]), from_before)
    later[...] = jnp.maximum(jnp.maximum(later_in[...], peaks[1:2, :]), from_after)


def call(kernel, outs, args, in_hbm=0, scratch=()):
    in_vmem = pl.BlockSpec(memory_space=pltpu.VMEM)
    return pl.pallas_call(
        kernel,
        out_shape=outs,
        in_specs=[pl.BlockSpec(memory_space=pl.ANY)] * in_hbm + [in_vmem] * (len(args) - in_hbm),
        out_specs=[in_vmem] * len(outs),
        scratch_shapes=scratch,
        compiler_params=pltpu.CompilerParams(vmem_limit_bytes=VMEM_LIMIT),
        cost_estimate=pl.CostEstimate(flops=1024, bytes_accessed=1024, transcendentals=0),
    )(*args)


def vectors(count, dtype=jnp.float32):
    return jax.ShapeDtypeStruct((count, ROWS), dtype)


def piece(rows):
    return jax.ShapeDtypeStruct((rows, WIDTH), jnp.bfloat16)


def per_device(embeddings, cluster_ids):
    ids = cluster_ids.reshape(1, ROWS)
    start, size = CHUNKS[0]
    cut = embeddings[start : start + size]
    got = [both_sides(cut)]
    (cut,) = call(
        noted_kernel,
        [piece(CHUNKS[1][1] + NOTE)],
        (embeddings, cut, ids),
        in_hbm=2,
        scratch=[pltpu.SemaphoreType.DMA],
    )
    got.append(both_sides(cut))
    normed, earlier, later, cut = call(
        own_kernel,
        [piece(ROWS), vectors(1), vectors(1), piece(CHUNKS[2][1])],
        (*got[0], embeddings, cluster_ids.reshape(ROWS, 1), ids),
        in_hbm=2,
    )
    got.append(both_sides(cut))
    sizes = [piece(size) for _, size in CHUNKS]
    *new, bounds, peaks, returned, cut = call(
        first_kernel,
        [*sizes[:2], *sizes[:2], vectors(8, jnp.int32), vectors(2), vectors(2), sizes[3]],
        (embeddings, *got[0], *got[1], normed, ids, earlier),
    )
    got.append(both_sides(cut))
    befores, afters = new[:2], new[2:]
    before, after, peaks, returned = call(
        functools.partial(next_kernel, 2),
        [sizes[2], sizes[2], vectors(2), vectors(2)],
        (*got[2], normed, bounds, peaks, returned, *befores, *afters),
    )
    befores.append(before)
    afters.append(after)
    before, after, returned = call(
        functools.partial(last_across_kernel, 3),
        [sizes[3], sizes[3], vectors(2)],
        (*got[3], bounds, returned, *befores, *afters),
    )
    sent_back = both_sides(returned)
    (peaks,) = call(
        functools.partial(last_own_kernel, 3),
        [vectors(2)],
        (before, after, normed, bounds, peaks),
    )
    earlier, later = call(
        join_kernel, [vectors(1), vectors(1)], (earlier, later, peaks, bounds, *sent_back)
    )
    return (earlier.reshape(ROWS), later.reshape(ROWS))


def solution(mesh):
    placed = (P(AXES, None), P(AXES))
    return jax.shard_map(
        per_device,
        mesh=mesh,
        in_specs=placed,
        out_specs=(P(AXES), P(AXES)),
        check_vma=False,
    )
```

time: 172 us -> 73.4 us (0.43)
  waiting for transfers between devices: 118 us -> 14.8 us
  matrix products: 16.1 us -> 0 us
  Pallas kernels: 0 us -> 15.8 us
  local copies, waits for them, and re-layouts: 0.01 us -> 5.43 us
  other arithmetic: 3.23 us -> 0 us
  starting transfers between devices: 33.7 us -> 36.2 us
    ppermute x8 -> x10, waiting for transfers between devices: 118 us -> 14.8 us  [exchanged(): return lax.ppermute(block, AXES, pairs + [(b, a) for a, b in pairs])]
    dot_general x5 -> x0, matrix products: 16.1 us -> none  [the longest x4 13.8 us: pair_peaks(): lax.dot_general(normed, other_rows, (((1,), (1,)), ((), ())), preferred_e...]
    pallas_call x0 -> x7, Pallas kernels: none -> 15.8 us  [call(): pl.pallas_call(kernel, out_shape=outs, in_specs=[pl.BlockSpec(memory_spac...]
    unnamed x4 -> x10, local copies, waits for them, and re-layouts: 0.01 us -> 3.32 us
    ppermute x8 -> x10, starting transfers between devices: 33.7 us -> 36.2 us  [exchanged(): return lax.ppermute(block, AXES, pairs + [(b, a) for a, b in pairs])]
    reduce_sum x1 -> x0, other arithmetic: 2.22 us -> none  [unit_rows(): jnp.sum(wide * wide, axis=1, keepdims=True) + 1e-06]
  transfers between devices with their start and end apart: 8 -> 10, of which waited for: 4 -> 4; matrix products, arithmetic and copies ran while one was open for 6% -> 1% of each run, Pallas kernels for 0% -> 19%
where the time goes in v2:
time: 73.4 us; the launch traced here: 73 us
  starting transfers between devices  36.2 us (49%)
  Pallas kernels  15.8 us (22%)
  waiting for transfers between devices  14.8 us (20%)
  local copies, waits for them, and re-layouts  5.43 us (7%)
  between operations  0.81 us (1%)
    ppermute x10, starting transfers between devices, exchanged(): return lax.ppermute(block, AXES, pairs + [(b, a) for a, b in pairs])  36.2 us
    pallas_call x7, Pallas kernels, call(): pl.pallas_call(kernel, out_shape=outs, in_specs=[pl.BlockSpec(memory_spac...  15.8 us
    ppermute x10, waiting for transfers between devices, exchanged(): return lax.ppermute(block, AXES, pairs + [(b, a) for a, b in pairs])  14.8 us
    unnamed x10, local copies, waits for them, and re-layouts  3.32 us
  transfers between devices with their start and end apart: 10, of which 4 were waited for; matrix products, arithmetic and copies ran while one was open for 1% of the time, Pallas kernels for 19%

profile of v2, /device:TPU:6, one launch (start us, length us, event | category | flops | bytes accessed | tf_op | source)
XLA Modules:
  0.0 73.0 jit_solution(6373750662632623371)
XLA Ops:
  0.6 0.0 copy-start.4
  0.6 1.1 %slice.3._ = bf16[256,1024]{1,0:T(8,128)(2,1)S(1)} slice(bf16[1024,1024]{1,0:T(8,128)(2,1)} %raw_ref.3), slice={[0:256], [0:1024]} | slice | bytes 1048576 | tf_op jit(solution)/shard_map/slice | solution.py:263
  1.7 2.0 %collective-permute-start = (bf16[256,1024]{1,0:T(8,128)(2,1)S(1)}, bf16[256,1024]{1,0:T(8,128)(2,1)S(1)}, u32[]{:S(2)}, u32[]{:S(2)}) collective-permute-start(bf16[256,1024]{1,0:T(8,128)(2,1)S(1)} %slice.3._), channel_id=1, source_target_pairs={{0,1},{2,3},{4,5},{6,7},{8,9},{10,11},{12,13},{14,15},{16,17},{18,... | collective-permute-start | bytes 1572872 | tf_op jit(solution)/shard_map/ppermute | solution.py:23
  3.7 8.7 %collective-permute-start.1 = (bf16[256,1024]{1,0:T(8,128)(2,1)S(1)}, bf16[256,1024]{1,0:T(8,128)(2,1)}, u32[]{:S(2)}, u32[]{:S(2)}) collective-permute-start(bf16[256,1024]{1,0:T(8,128)(2,1)S(1)} %slice.3._), channel_id=1, source_target_pairs={{1,2},{3,4},{5,6},{7,8},{9,10},{11,12},{13,14},{15,16},{17,18},{19... | collective-permute-start | bytes 1572872 | tf_op jit(solution)/shard_map/ppermute | solution.py:23
  12.5 0.0 copy-start
  12.5 1.6 %copy-done = bf16[1024,1024]{1,0:T(8,128)(2,1)S(1)} copy-done((bf16[1024,1024]{1,0:T(8,128)(2,1)S(1)}, bf16[1024,1024]{1,0:T(8,128)(2,1)}, u32[]{:S(2)}) %copy-start) | copy-done | bytes 2097176
  14.1 0.0 copy-start.3
  14.1 0.7 copy-done.3
  14.7 0.0 copy-start.1
  14.7 1.0 %shard_map.42 = bf16[272,1024]{1,0:T(8,128)(2,1)} custom-call(bf16[1024,1024]{1,0:T(8,128)(2,1)S(1)} %copy-done, bf16[256,1024]{1,0:T(8,128)(2,1)S(1)} %slice.3._, s32[1,1024]{1,0:T(1,128)S(1)} %bitcast.4), custom_call_target="tpu_custom_call" | custom-call | flops 1024 | bytes 1024 | tf_op jit(solution)/shard_map/pallas_call | solution.py:241
  15.8 0.1 collective-permute-start.2
  15.9 3.3 %collective-permute-start.3 = (bf16[272,1024]{1,0:T(8,128)(2,1)}, bf16[272,1024]{1,0:T(8,128)(2,1)}, u32[]{:S(2)}, u32[]{:S(2)}) collective-permute-start(bf16[272,1024]{1,0:T(8,128)(2,1)} %shard_map.42), channel_id=1, source_target_pairs={{1,2},{3,4},{5,6},{7,8},{9,10},{11,12},{13,14},{15,16},{17,18},{19... | collective-permute-start | bytes 1671176 | tf_op jit(solution)/shard_map/ppermute | solution.py:23
  19.2 0.0 copy-done.4
  19.2 1.0 %copy.4.row_ids_ref = s32[1024,1]{1,0:T(8,128)} copy(s32[1024,1]{0,1:T(1,128)S(1)} %bitcast.5) | data formatting | bytes 8192 | tf_op jit(solution)/shard_map/reshape | solution.py:276
  20.3 0.0 collective-permute-done._.refs_0_
  20.3 4.8 %collective-permute-done.1.__.refs_1_ = bf16[256,1024]{1,0:T(8,128)(2,1)} collective-permute-done((bf16[256,1024]{1,0:T(8,128)(2,1)S(1)}, bf16[256,1024]{1,0:T(8,128)(2,1)}, u32[]{:S(2)}, u32[]{:S(2)}) %collective-permute-start.1) | collective-permute-done | bytes 524320 | tf_op jit(solution)/shard_map/ppermute | solution.py:23
  25.0 0.0 copy-done.1
  25.0 0.0 copy-start.2
  25.0 1.0 %copy-done.2 = s32[1024,1]{1,0:T(8,128)S(1)} copy-done((s32[1024,1]{1,0:T(8,128)S(1)}, s32[1024,1]{1,0:T(8,128)}, u32[]{:S(2)}) %copy-start.2) | copy-done | bytes 4120
  26.1 3.0 %shard_map.41 = (bf16[1024,1024]{1,0:T(8,128)(2,1)S(1)}, f32[1,1024]{1,0:T(1,128)S(1)}, f32[1,1024]{1,0:T(1,128)S(1)}, bf16[384,1024]{1,0:T(8,128)(2,1)S(1)}) custom-call(bf16[256,1024]{1,0:T(8,128)(2,1)S(1)} %collective-permute-done._.refs_0_, bf16[256,1024]{1,0:T(8,128)(2,1)} %collective-permute-done.1.__.refs_1_, bf16[1024,1024]{1,0:T(8,128)(2,1)S(1)} %copy-done.1, ...), custom_call_target="tpu_custom_call" | custom-call | flops 1024 | bytes 1024 | tf_op jit(solution)/shard_map/pallas_call | solution.py:241
  29.1 0.1 collective-permute-start.6
  29.2 7.9 %collective-permute-start.7 = (bf16[384,1024]{1,0:T(8,128)(2,1)S(1)}, bf16[384,1024]{1,0:T(8,128)(2,1)S(1)}, u32[]{:S(2)}, u32[]{:S(2)}) collective-permute-start(bf16[384,1024]{1,0:T(8,128)(2,1)S(1)} %get-tuple-element.28), channel_id=1, source_target_pairs={{1,2},{3,4},{5,6},{7,8},{9,10},{11,12},{13,14},{15,16},{17,18},{19... | collective-permute-start | bytes 2359304 | tf_op jit(solution)/shard_map/ppermute | solution.py:23
  37.1 0.0 collective-permute-done.2.refs_2_
  37.1 0.1 collective-permute-done.3.refs_3_
  37.2 5.1 %shard_map.43 = (bf16[256,1024]{1,0:T(8,128)(2,1)S(1)}, bf16[256,1024]{1,0:T(8,128)(2,1)S(1)}, bf16[256,1024]{1,0:T(8,128)(2,1)S(1)}, bf16[256,1024]{1,0:T(8,128...) custom-call(bf16[1024,1024]{1,0:T(8,128)(2,1)S(1)} %copy-done.1, ...), custom_call_target="tpu_custom_call" | custom-call | flops 1024 | bytes 1024 | tf_op jit(solution)/shard_map/pallas_call | solution.py:241
  42.3 0.1 collective-permute-start.4
  42.4 7.8 %collective-permute-start.5 = (bf16[128,1024]{1,0:T(8,128)(2,1)S(1)}, bf16[128,1024]{1,0:T(8,128)(2,1)S(1)}, u32[]{:S(2)}, u32[]{:S(2)}) collective-permute-start(bf16[128,1024]{1,0:T(8,128)(2,1)S(1)} %get-tuple-element.26), channel_id=1, source_target_pairs={{1,2},{3,4},{5,6},{7,8},{9,10},{11,12},{13,14},{15,16},{17,18},{19... | collective-permute-start | bytes 786440 | tf_op jit(solution)/shard_map/ppermute | solution.py:23
  50.3 0.0 collective-permute-done.6.side_0
  50.3 7.5 %collective-permute-done.7.side_1 = bf16[384,1024]{1,0:T(8,128)(2,1)S(1)} collective-permute-done((bf16[384,1024]{1,0:T(8,128)(2,1)S(1)}, bf16[384,1024]{1,0:T(8,128)(2,1)S(1)}, u32[]{:S(2)}, u32[]{:S(2)}) %collective-permute-start.7) | collective-permute-done | bytes 786464 | tf_op jit(solution)/shard_map/ppermute | solution.py:23
  57.8 3.9 %shard_map.44 = (bf16[384,1024]{1,0:T(8,128)(2,1)S(1)}, bf16[384,1024]{1,0:T(8,128)(2,1)S(1)}, f32[2,1024]{1,0:T(2,128)S(1)}, f32[2,1024]{1,0:T(2,128)S(1)}) custom-call(bf16[384,1024]{1,0:T(8,128)(2,1)S(1)} %collective-permute-done.6.side_0, bf16[384,1024]{1,0:T(8,128)(2,1)S(1)} %collective-permute-done.7.side_1, ...), custom_call_target="tpu_custom_call" | custom-call | flops 1024 | bytes 1024 | tf_op jit(solution)/shard_map/pallas_call | solution.py:241
  61.7 0.0 collective-permute-done.4.side_0
  61.7 0.0 collective-permute-done.5.side_1
  61.7 1.4 %shard_map.45 = (bf16[128,1024]{1,0:T(8,128)(2,1)S(1)}, bf16[128,1024]{1,0:T(8,128)(2,1)S(1)}, f32[2,1024]{1,0:T(2,128)S(1)}) custom-call(bf16[128,1024]{1,0:T(8,128)(2,1)S(1)} %collective-permute-done.4.side_0, bf16[128,1024]{1,0:T(8,128)(2,1)S(1)} %collective-permute-done.5.side_1, s32[8,1024]{1,0:T(8,128)S(1)} %get-tuple-element.27.bounds, ...), custom_call_target="tpu_custom_call" | custom-call | flops 1024 | bytes 1024 | tf_op jit(solution)/shard_map/pallas_call | solution.py:241
  63.1 0.1 collective-permute-start.8
  63.2 6.0 %collective-permute-start.9 = (f32[2,1024]{1,0:T(2,128)S(1)}, f32[2,1024]{1,0:T(2,128)S(1)}, u32[]{:S(2)}, u32[]{:S(2)}) collective-permute-start(f32[2,1024]{1,0:T(2,128)S(1)} %get-tuple-element.41), channel_id=1, source_target_pairs={{1,2},{3,4},{5,6},{7,8},{9,10},{11,12},{13,14},{15,16},{17,18},{19... | collective-permute-start | bytes 24584 | tf_op jit(solution)/shard_map/ppermute | solution.py:23
  69.3 0.8 %shard_map.46.peaks = f32[2,1024]{1,0:T(2,128)S(1)} custom-call(bf16[128,1024]{1,0:T(8,128)(2,1)S(1)} %get-tuple-element.38.before, bf16[128,1024]{1,0:T(8,128)(2,1)S(1)} %get-tuple-element.39.after, bf16[1024,1024]{1,0:T(8,128)(2,1)S(1)} %get-tuple-element.25.refs_4_.normed, s32[8,1024]{1,0:T(8,128)S(1)} %get-tuple-element.27.bounds, ...), custom_call_target="tpu_custom_call" | custom-call | flops 1024 | bytes 1024 | tf_op jit(solution)/shard_map/pallas_call | solution.py:241
  70.0 0.0 collective-permute-done.8.side_0
  70.0 2.4 %collective-permute-done.9.side_1 = f32[2,1024]{1,0:T(2,128)S(1)} collective-permute-done((f32[2,1024]{1,0:T(2,128)S(1)}, f32[2,1024]{1,0:T(2,128)S(1)}, u32[]{:S(2)}, u32[]{:S(2)}) %collective-permute-start.9) | collective-permute-done | bytes 8224 | tf_op jit(solution)/shard_map/ppermute | solution.py:23
  72.4 0.6 shard_map.47
Async XLA Ops:
  0.6 18.6 %copy-start.4 = (s32[1024]{0:T(1024)S(1)}, s32[1024]{0:T(1024)}, u32[]{:S(2)}) copy-start(s32[1024]{0:T(1024)} %param.3) | copy-start | bytes 12292
  1.7 18.5 %collective-permute-start = (bf16[256,1024]{1,0:T(8,128)(2,1)S(1)}, bf16[256,1024]{1,0:T(8,128)(2,1)S(1)}, u32[]{:S(2)}, u32[]{:S(2)}) collective-permute-start(bf16[256,1024]{1,0:T(8,128)(2,1)S(1)} %slice.3._), channel_id=1, source_target_pairs={{0,1},{2,3},{4,5},{6,7},{8,9},{10,11},{12,13},{14,15},{16,17},{18,... | collective-permute-start | bytes 1572872 | tf_op jit(solution)/shard_map/ppermute | solution.py:23
  3.7 21.3 %collective-permute-start.1 = (bf16[256,1024]{1,0:T(8,128)(2,1)S(1)}, bf16[256,1024]{1,0:T(8,128)(2,1)}, u32[]{:S(2)}, u32[]{:S(2)}) collective-permute-start(bf16[256,1024]{1,0:T(8,128)(2,1)S(1)} %slice.3._), channel_id=1, source_target_pairs={{1,2},{3,4},{5,6},{7,8},{9,10},{11,12},{13,14},{15,16},{17,18},{19... | collective-permute-start | bytes 1572872 | tf_op jit(solution)/shard_map/ppermute | solution.py:23
  12.5 1.6 %copy-start = (bf16[1024,1024]{1,0:T(8,128)(2,1)S(1)}, bf16[1024,1024]{1,0:T(8,128)(2,1)}, u32[]{:S(2)}) copy-start(bf16[1024,1024]{1,0:T(8,128)(2,1)} %raw_ref.3) | copy-start | bytes 6291460
  14.1 0.7 copy-start.3
  14.7 10.3 %copy-start.1 = (bf16[1024,1024]{1,0:T(8,128)(2,1)S(1)}, bf16[1024,1024]{1,0:T(8,128)(2,1)}, u32[]{:S(2)}) copy-start(bf16[1024,1024]{1,0:T(8,128)(2,1)} %raw_ref.3) | copy-start | bytes 6291460
  15.8 21.3 %collective-permute-start.2 = (bf16[272,1024]{1,0:T(8,128)(2,1)}, bf16[272,1024]{1,0:T(8,128)(2,1)}, u32[]{:S(2)}, u32[]{:S(2)}) collective-permute-start(bf16[272,1024]{1,0:T(8,128)(2,1)} %shard_map.42), channel_id=1, source_target_pairs={{0,1},{2,3},{4,5},{6,7},{8,9},{10,11},{12,13},{14,15},{16,17},{18,... | collective-permute-start | bytes 1671176 | tf_op jit(solution)/shard_map/ppermute | solution.py:23
  15.9 21.3 %collective-permute-start.3 = (bf16[272,1024]{1,0:T(8,128)(2,1)}, bf16[272,1024]{1,0:T(8,128)(2,1)}, u32[]{:S(2)}, u32[]{:S(2)}) collective-permute-start(bf16[272,1024]{1,0:T(8,128)(2,1)} %shard_map.42), channel_id=1, source_target_pairs={{1,2},{3,4},{5,6},{7,8},{9,10},{11,12},{13,14},{15,16},{17,18},{19... | collective-permute-start | bytes 1671176 | tf_op jit(solution)/shard_map/ppermute | solution.py:23
  25.0 1.0 %copy-start.2 = (s32[1024,1]{1,0:T(8,128)S(1)}, s32[1024,1]{1,0:T(8,128)}, u32[]{:S(2)}) copy-start(s32[1024,1]{1,0:T(8,128)} %copy.4.row_ids_ref) | copy-start | bytes 12292
  29.1 21.2 %collective-permute-start.6 = (bf16[384,1024]{1,0:T(8,128)(2,1)S(1)}, bf16[384,1024]{1,0:T(8,128)(2,1)S(1)}, u32[]{:S(2)}, u32[]{:S(2)}) collective-permute-start(bf16[384,1024]{1,0:T(8,128)(2,1)S(1)} %get-tuple-element.28), channel_id=1, source_target_pairs={{0,1},{2,3},{4,5},{6,7},{8,9},{10,11},{12,13},{14,15},{16,17},{18,... | collective-permute-start | bytes 2359304 | tf_op jit(solution)/shard_map/ppermute | solution.py:23
  29.2 28.6 %collective-permute-start.7 = (bf16[384,1024]{1,0:T(8,128)(2,1)S(1)}, bf16[384,1024]{1,0:T(8,128)(2,1)S(1)}, u32[]{:S(2)}, u32[]{:S(2)}) collective-permute-start(bf16[384,1024]{1,0:T(8,128)(2,1)S(1)} %get-tuple-element.28), channel_id=1, source_target_pairs={{1,2},{3,4},{5,6},{7,8},{9,10},{11,12},{13,14},{15,16},{17,18},{19... | collective-permute-start | bytes 2359304 | tf_op jit(solution)/shard_map/ppermute | solution.py:23
  42.3 19.3 %collective-permute-start.4 = (bf16[128,1024]{1,0:T(8,128)(2,1)S(1)}, bf16[128,1024]{1,0:T(8,128)(2,1)S(1)}, u32[]{:S(2)}, u32[]{:S(2)}) collective-permute-start(bf16[128,1024]{1,0:T(8,128)(2,1)S(1)} %get-tuple-element.26), channel_id=1, source_target_pairs={{0,1},{2,3},{4,5},{6,7},{8,9},{10,11},{12,13},{14,15},{16,17},{18,... | collective-permute-start | bytes 786440 | tf_op jit(solution)/shard_map/ppermute | solution.py:23
  42.4 19.2 %collective-permute-start.5 = (bf16[128,1024]{1,0:T(8,128)(2,1)S(1)}, bf16[128,1024]{1,0:T(8,128)(2,1)S(1)}, u32[]{:S(2)}, u32[]{:S(2)}) collective-permute-start(bf16[128,1024]{1,0:T(8,128)(2,1)S(1)} %get-tuple-element.26), channel_id=1, source_target_pairs={{1,2},{3,4},{5,6},{7,8},{9,10},{11,12},{13,14},{15,16},{17,18},{19... | collective-permute-start | bytes 786440 | tf_op jit(solution)/shard_map/ppermute | solution.py:23
  63.1 6.9 %collective-permute-start.8 = (f32[2,1024]{1,0:T(2,128)S(1)}, f32[2,1024]{1,0:T(2,128)S(1)}, u32[]{:S(2)}, u32[]{:S(2)}) collective-permute-start(f32[2,1024]{1,0:T(2,128)S(1)} %get-tuple-element.41), channel_id=1, source_target_pairs={{0,1},{2,3},{4,5},{6,7},{8,9},{10,11},{12,13},{14,15},{16,17},{18,... | collective-permute-start | bytes 24584 | tf_op jit(solution)/shard_map/ppermute | solution.py:23
  63.2 9.2 %collective-permute-start.9 = (f32[2,1024]{1,0:T(2,128)S(1)}, f32[2,1024]{1,0:T(2,128)S(1)}, u32[]{:S(2)}, u32[]{:S(2)}) collective-permute-start(f32[2,1024]{1,0:T(2,128)S(1)} %get-tuple-element.41), channel_id=1, source_target_pairs={{1,2},{3,4},{5,6},{7,8},{9,10},{11,12},{13,14},{15,16},{17,18},{19... | collective-permute-start | bytes 24584 | tf_op jit(solution)/shard_map/ppermute | solution.py:23

commit v3 on v2

v3 whole, which is shorter than its diff:
```python
import functools

import jax
import jax.numpy as jnp
from jax import lax
from jax.experimental import pallas as pl
from jax.experimental.pallas import tpu as pltpu
from jax.sharding import PartitionSpec as P

ROWS = 1024
WIDTH = 1024
TILE = 256
EDGE = 128
TO_AFTER = ((256, 256), (128, 128), (ROWS - EDGE, EDGE), (512, 384), (0, EDGE))
TO_BEFORE = ((256, 256), (128, 128), (0, EDGE), (512, 384), (ROWS - EDGE, EDGE))
SIZES = tuple(size for _, size in TO_AFTER)
NOTE = 16
RADIX = 32
VMEM_LIMIT = 16 * 1024 * 1024
AXES = ("group", "dev")


def exchanged(*blocks):
    devices = lax.axis_size(AXES)
    got = []
    for side, block in enumerate(blocks):
        pairs = [(i, i + 1) for i in range(side, devices - 1, 2)]
        got.append(lax.ppermute(block, AXES, pairs + [(b, a) for a, b in pairs]))
    return got


def faces_after(side):
    return lax.axis_index("dev") % 2 == side


def by_role(side_0, side_1):
    odd = lax.axis_index("dev") % 2 == 1
    return jnp.where(odd, side_0, side_1), jnp.where(odd, side_1, side_0)


def unit_rows(values):
    wide = values.astype(jnp.float32)
    return (wide * lax.rsqrt(jnp.sum(wide * wide, axis=1, keepdims=True) + 1e-06)).astype(
        jnp.bfloat16
    )


def products(rows, columns):
    return lax.dot_general(
        rows, columns, (((1,), (1,)), ((), ())), preferred_element_type=jnp.float32
    )


def places(shape, axis):
    return lax.broadcasted_iota(jnp.int32, shape, axis)


def best_allowed(allowed, scores):
    return jnp.max(jnp.where(allowed, scores, -1.0), axis=0, keepdims=True)


def raise_peak(peaks_ref, row, at, best):
    row = slice(row, row + 1)
    peaks_ref[row, at] = jnp.maximum(peaks_ref[row, at], best)


def edge_run(ids, edge):
    label = ids[:, edge : edge + 1]
    return label, jnp.sum((ids == label).astype(jnp.int32), axis=1, keepdims=True)


def written_note(ids):
    row = places((NOTE, WIDTH), 0)
    note = jnp.zeros((NOTE, WIDTH), jnp.int32)
    for k, edge in enumerate((0, ROWS - 1)):
        label, count = edge_run(ids, edge)
        for n, value in enumerate((label, count // RADIX, count % RADIX)):
            note = jnp.where(row == 3 * k + n, value, note)
    return note.astype(jnp.float32).astype(jnp.bfloat16)


def read_note(note, k):
    note = note.astype(jnp.float32).astype(jnp.int32)
    label, high, low = (note[3 * k + n : 3 * k + n + 1, 0:1] for n in range(3))
    return label, high * RADIX + low


def cut_copy(raw_hbm, chunk, side, piece_ref, sem):
    (low, size), (other_low, _) = TO_AFTER[chunk], TO_BEFORE[chunk]
    if low != other_low:
        low = pl.multiple_of(jnp.where(faces_after(side), low, other_low), EDGE)
    copy = pltpu.make_async_copy(raw_hbm.at[pl.ds(low, size)], piece_ref, sem)
    copy.start()
    return copy


def noted_kernel(raw_hbm, _, ids_ref, *refs):
    pieces, sems = refs[:2], refs[2]
    copies = []
    for side in range(2):
        for k, chunk in enumerate((1, 2)):
            rows = pieces[side].at[pl.ds(k * EDGE, EDGE)]
            copies.append(cut_copy(raw_hbm, chunk, side, rows, sems.at[2 * side + k]))
    note = written_note(ids_ref[...])
    for piece_ref in pieces:
        piece_ref[2 * EDGE :, :] = note
    for copy in copies:
        copy.wait()


def middle_kernel(raw_hbm, _, __, piece_ref, sem):
    cut_copy(raw_hbm, 3, 0, piece_ref, sem).wait()


def own_kernel(raw_ref, row_ids_ref, ids_ref, normed_ref, earlier_ref, later_ref):
    for part in range(0, ROWS, 128):
        normed_ref[part : part + 128, :] = unit_rows(raw_ref[part : part + 128, :])
    earlier_ref[...] = jnp.full_like(earlier_ref, -1.0)
    later_ref[...] = jnp.full_like(later_ref, -1.0)
    tiles = ROWS // TILE
    for row_tile in range(tiles):
        rows_at = pl.ds(row_tile * TILE, TILE)
        rows = normed_ref[rows_at, :]
        for tile in range(tiles):
            at = pl.ds(tile * TILE, TILE)
            scores = products(rows, normed_ref[at, :])
            shared = row_ids_ref[rows_at, :] == ids_ref[:, at]
            row, column = places(shared.shape, 0), places(shared.shape, 1)
            if row_tile <= tile:
                allowed = shared & (row < column) if row_tile == tile else shared
                raise_peak(earlier_ref, 0, at, best_allowed(allowed, scores))
            if row_tile >= tile:
                allowed = shared & (row > column) if row_tile == tile else shared
                raise_peak(later_ref, 0, at, best_allowed(allowed, scores))


OWN_BEFORE, OWN_AFTER, AFTER_BEFORE = range(3)
COUNT_BEFORE, COUNT_AFTER, OWN_HEAD, OWN_TAIL = range(4, 8)


def find_bounds(ids, note_before, note_after, bounds):
    (label_before, count_before) = read_note(note_before, 1)
    (label_after, count_after) = read_note(note_after, 0)
    first_before = ROWS - count_before
    joined = label_before == label_after
    place = places((1, ROWS), 1)
    rows = {
        OWN_BEFORE: jnp.where(ids == label_before, first_before, ROWS),
        OWN_AFTER: jnp.where(ids == label_after, count_after, 0),
        AFTER_BEFORE: jnp.where(joined & (place < count_after), first_before, ROWS),
    }
    own_head = jnp.sum((ids == label_before).astype(jnp.int32), axis=1, keepdims=True)
    own_tail = jnp.sum((ids == label_after).astype(jnp.int32), axis=1, keepdims=True)
    counts = (COUNT_BEFORE, count_before), (COUNT_AFTER, count_after)
    for row, count in (*counts, (OWN_HEAD, own_head), (OWN_TAIL, own_tail)):
        rows[row] = jnp.broadcast_to(count, (1, ROWS))
    for row, value in rows.items():
        bounds[row : row + 1, :] = value


def read_counts(bounds):
    return [jnp.max(bounds[row : row + 1, :128]) for row in range(4, 8)]


def against_own(chunk, before, after, normed_ref, bounds, peaks):
    size = SIZES[chunk]
    low_before, low_after = TO_AFTER[chunk][0], TO_BEFORE[chunk][0]
    tiles = [pl.ds(tile * TILE, TILE) for tile in range(ROWS // TILE)]

    def raise_own(row, at, scores):
        place = places(scores.shape, 0) + (low_after if row else low_before)
        bound = bounds[OWN_BEFORE + row : OWN_BEFORE + row + 1, at]
        allowed = (place < bound) if row else (place >= bound)
        raise_peak(peaks, row, at, best_allowed(allowed, scores))

    if size < TILE:
        rows = jnp.concatenate([before[...], after[...]], axis=0)
        for at in tiles:
            scores = products(rows, normed_ref[at, :])
            raise_own(0, at, scores[:size])
            raise_own(1, at, scores[size:])
        return
    count_before, count_after, own_head, own_tail = read_counts(bounds)

    @pl.when((ROWS - count_before < low_before + size) & (own_head > 0))
    def _():
        for at in tiles:
            raise_own(0, at, products(before[...], normed_ref[at, :]))

    @pl.when((count_after > low_after) & (own_tail > 0))
    def _():
        for at in tiles:
            raise_own(1, at, products(after[...], normed_ref[at, :]))


def across(chunk, befores, afters, bounds, returned):
    _, _, own_head, own_tail = read_counts(bounds)

    @pl.when((own_head == ROWS) & (own_tail == ROWS))
    def _():
        for i in range(chunk + 1):
            for j in range(chunk + 1):
                if max(i, j) == chunk:
                    across_pieces(befores[i], *TO_AFTER[i], afters[j], *TO_BEFORE[j], bounds, returned)


def across_pieces(before, low_i, size_i, after, low_j, size_j, bounds, returned):
    skip_i = max(0, low_j - low_i)
    size_j = min(size_j, low_i + size_i - low_j)
    if skip_i >= size_i or size_j <= 0:
        return
    low_i, size_i = low_i + skip_i, size_i - skip_i
    rows = before[skip_i : skip_i + size_i, :]
    best = jnp.full((size_i, 128), -1.0, jnp.float32)
    for part in range(0, size_j, TILE):
        size = min(TILE, size_j - part)
        at = pl.ds(low_j + part, size)
        scores = products(rows, after[part : part + size, :])
        bound = bounds[AFTER_BEFORE : AFTER_BEFORE + 1, at]
        masked = jnp.where(places(scores.shape, 0) + low_i >= bound, scores, -1.0)
        raise_peak(returned, 1, at, jnp.max(masked, axis=0, keepdims=True))
        for lanes in range(0, size, 128):
            best = jnp.maximum(best, masked[:, lanes : lanes + 128])
    raise_peak(returned, 0, pl.ds(low_i, size_i), jnp.max(best.T, axis=0, keepdims=True))


def take_chunk(side_0, side_1, before, after):
    for part in range(0, before.shape[0], 128):
        at = slice(part, part + 128)
        before[at, :], after[at, :] = by_role(unit_rows(side_0[at, :]), unit_rows(side_1[at, :]))


def first_kernel(raw_hbm, *refs):
    (first, noted), (normed, ids_ref, _) = (refs[0:2], refs[2:4]), refs[4:7]
    befores, afters = refs[7:10], refs[10:13]
    bounds, peaks, returned = refs[13:16]
    pieces, sems = refs[16:18], refs[18]
    copies = [cut_copy(raw_hbm, 4, side, pieces[side], sems.at[side]) for side in range(2)]
    peaks[...] = jnp.full_like(peaks, -1.0)
    returned[...] = jnp.full_like(returned, -1.0)
    notes = by_role(*(side[2 * EDGE :, :128].astype(jnp.float32) for side in noted))
    find_bounds(ids_ref[...], *notes, bounds)
    got = first, [side.at[pl.ds(0, EDGE)] for side in noted], [side.at[pl.ds(EDGE, EDGE)] for side in noted]
    for chunk in range(3):
        take_chunk(*got[chunk], befores[chunk], afters[chunk])
        against_own(chunk, befores[chunk], afters[chunk], normed, bounds, peaks)
        across(chunk, befores, afters, bounds, returned)
    for copy in copies:
        copy.wait()


def next_kernel(chunk, side_0, side_1, normed, bounds, peaks_in, returned_in, *refs):
    befores, afters = refs[:chunk], refs[chunk : 2 * chunk]
    before, after, peaks, returned = refs[2 * chunk :]
    peaks[...] = peaks_in[...]
    returned[...] = returned_in[...]
    take_chunk(side_0, side_1, before, after)
    against_own(chunk, before, after, normed, bounds, peaks)
    across(chunk, [*befores, before], [*afters, after], bounds, returned)


def last_across_kernel(chunk, side_0, side_1, bounds, returned_in, *refs):
    befores, afters = refs[:chunk], refs[chunk : 2 * chunk]
    before, after, returned = refs[2 * chunk :]
    returned[...] = returned_in[...]
    take_chunk(side_0, side_1, before, after)
    across(chunk, [*befores, before], [*afters, after], bounds, returned)


def last_own_kernel(chunk, before, after, normed, bounds, peaks_in, peaks):
    peaks[...] = peaks_in[...]
    against_own(chunk, before, after, normed, bounds, peaks)


def join_kernel(earlier_in, later_in, peaks, bounds, side_0, side_1, earlier, later):
    from_before, from_after = by_role(side_0[...], side_1[...])
    has_before = bounds[COUNT_BEFORE : COUNT_BEFORE + 1, :] > 0
    has_after = bounds[COUNT_AFTER : COUNT_AFTER + 1, :] > 0
    from_before = jnp.where(has_before, from_before[1:2], -1.0)
    from_after = jnp.where(has_after, from_after[0:1], -1.0)
    earlier[...] = jnp.maximum(jnp.maximum(earlier_in[...], peaks[0:1, :]), from_before)
    later[...] = jnp.maximum(jnp.maximum(later_in[...], peaks[1:2, :]), from_after)


def call(kernel, outs, args, in_hbm=0, scratch=()):
    in_vmem = pl.BlockSpec(memory_space=pltpu.VMEM)
    return pl.pallas_call(
        kernel,
        out_shape=outs,
        in_specs=[pl.BlockSpec(memory_space=pl.ANY)] * in_hbm + [in_vmem] * (len(args) - in_hbm),
        out_specs=[in_vmem] * len(outs),
        scratch_shapes=scratch,
        compiler_params=pltpu.CompilerParams(vmem_limit_bytes=VMEM_LIMIT),
        cost_estimate=pl.CostEstimate(flops=1024, bytes_accessed=1024, transcendentals=0),
    )(*args)


def vectors(count, dtype=jnp.float32):
    return jax.ShapeDtypeStruct((count, ROWS), dtype)


def piece(rows):
    return jax.ShapeDtypeStruct((rows, WIDTH), jnp.bfloat16)


def per_device(embeddings, cluster_ids):
    ids = cluster_ids.reshape(1, ROWS)
    low, size = TO_AFTER[0]
    cut = embeddings[low : low + size]
    first = exchanged(cut, cut)
    cuts = call(
        noted_kernel,
        [piece(2 * EDGE + NOTE)] * 2,
        (embeddings, cut, ids),
        in_hbm=2,
        scratch=[pltpu.SemaphoreType.DMA((4,))],
    )
    noted = exchanged(*cuts)
    (cut,) = call(
        middle_kernel,
        [piece(SIZES[3])],
        (embeddings, *first),
        in_hbm=3,
        scratch=[pltpu.SemaphoreType.DMA],
    )
    middle = exchanged(cut, cut)
    normed, earlier, later = call(
        own_kernel,
        [piece(ROWS), vectors(1), vectors(1)],
        (embeddings, cluster_ids.reshape(ROWS, 1), ids),
    )
    sizes = [piece(size) for size in SIZES]
    *new, bounds, peaks, returned, cut_0, cut_1 = call(
        first_kernel,
        [*sizes[:3], *sizes[:3], vectors(8, jnp.int32), vectors(2), vectors(2), sizes[4], sizes[4]],
        (embeddings, *first, *noted, normed, ids, earlier),
        in_hbm=1,
        scratch=[pltpu.SemaphoreType.DMA((2,))],
    )
    last = exchanged(cut_0, cut_1)
    befores, afters = new[:3], new[3:]
    before, after, peaks, returned = call(
        functools.partial(next_kernel, 3),
        [sizes[3], sizes[3], vectors(2), vectors(2)],
        (*middle, normed, bounds, peaks, returned, *befores, *afters),
    )
    befores.append(before)
    afters.append(after)
    before, after, returned = call(
        functools.partial(last_across_kernel, 4),
        [sizes[4], sizes[4], vectors(2)],
        (*last, bounds, returned, *befores, *afters),
    )
    sent_back = exchanged(returned, returned)
    (peaks,) = call(
        functools.partial(last_own_kernel, 4),
        [vectors(2)],
        (before, after, normed, bounds, peaks),
    )
    earlier, later = call(
        join_kernel, [vectors(1), vectors(1)], (earlier, later, peaks, bounds, *sent_back)
    )
    return (earlier.reshape(ROWS), later.reshape(ROWS))


def solution(mesh):
    placed = (P(AXES, None), P(AXES))
    return jax.shard_map(
        per_device,
        mesh=mesh,
        in_specs=placed,
        out_specs=(P(AXES), P(AXES)),
        check_vma=False,
    )
```

time: 73.4 us -> 71.8 us (0.978)
  starting transfers between devices: 36.2 us -> 33.5 us
    ppermute x10, starting transfers between devices: 36.2 us -> 33.5 us  [exchanged(): got.append(lax.ppermute(block, AXES, pairs + [(b, a) for a, b in pairs]))]
    ppermute x10, waiting for transfers between devices: 14.8 us -> 15.5 us  [exchanged(): got.append(lax.ppermute(block, AXES, pairs + [(b, a) for a, b in pairs]))]
    pallas_call x7 -> x8, Pallas kernels: 15.8 us -> 15.9 us  [call(): pl.pallas_call(kernel, out_shape=outs, in_specs=[pl.BlockSpec(memory_spac...]
  transfers between devices with their start and end apart: 10 -> 10, of which waited for: 4 -> 4; matrix products, arithmetic and copies ran while one was open for 1% -> 1% of each run, Pallas kernels for 19% -> 21%
where the time goes in v3:
time: 71.8 us; the launch traced here: 71.2 us
  starting transfers between devices  33.5 us (47%)
  Pallas kernels  15.9 us (22%)
  waiting for transfers between devices  15.5 us (22%)
  local copies, waits for them, and re-layouts  5.44 us (8%)
  between operations  0.84 us (1%)
    ppermute x10, starting transfers between devices, exchanged(): got.append(lax.ppermute(block, AXES, pairs + [(b, a) for a, b in pairs]))  33.5 us
    pallas_call x8, Pallas kernels, call(): pl.pallas_call(kernel, out_shape=outs, in_specs=[pl.BlockSpec(memory_spac...  15.9 us
    ppermute x10, waiting for transfers between devices, exchanged(): got.append(lax.ppermute(block, AXES, pairs + [(b, a) for a, b in pairs]))  15.5 us
    unnamed x10, local copies, waits for them, and re-layouts  3.33 us
  transfers between devices with their start and end apart: 10, of which 4 were waited for; matrix products, arithmetic and copies ran while one was open for 1% of the time, Pallas kernels for 21%

profile of v3, /device:TPU:6, one launch (start us, length us, event | category | flops | bytes accessed | tf_op | source)
XLA Modules:
  0.0 71.2 jit_solution(15497165002858861220)
XLA Ops:
  0.6 1.1 %slice.3._ = bf16[256,1024]{1,0:T(8,128)(2,1)S(1)} slice(bf16[1024,1024]{1,0:T(8,128)(2,1)} %raw_hbm.5), slice={[256:512], [0:1024]} | slice | bytes 1048576 | tf_op jit(solution)/shard_map/slice | solution.py:309
  1.7 2.0 %collective-permute-start = (bf16[256,1024]{1,0:T(8,128)(2,1)S(1)}, bf16[256,1024]{1,0:T(8,128)(2,1)S(1)}, u32[]{:S(2)}, u32[]{:S(2)}) collective-permute-start(bf16[256,1024]{1,0:T(8,128)(2,1)S(1)} %slice.3._), channel_id=1, source_target_pairs={{0,1},{2,3},{4,5},{6,7},{8,9},{10,11},{12,13},{14,15},{16,17},{18,... | collective-permute-start | bytes 1572872 | tf_op jit(solution)/shard_map/ppermute | solution.py:28
  3.7 8.7 %collective-permute-start.1 = (bf16[256,1024]{1,0:T(8,128)(2,1)S(1)}, bf16[256,1024]{1,0:T(8,128)(2,1)S(1)}, u32[]{:S(2)}, u32[]{:S(2)}) collective-permute-start(bf16[256,1024]{1,0:T(8,128)(2,1)S(1)} %slice.3._), channel_id=1, source_target_pairs={{1,2},{3,4},{5,6},{7,8},{9,10},{11,12},{13,14},{15,16},{17,18},{19... | collective-permute-start | bytes 1572872 | tf_op jit(solution)/shard_map/ppermute | solution.py:28
  12.4 0.0 copy-start
  12.5 1.6 %copy-done = bf16[1024,1024]{1,0:T(8,128)(2,1)S(1)} copy-done((bf16[1024,1024]{1,0:T(8,128)(2,1)S(1)}, bf16[1024,1024]{1,0:T(8,128)(2,1)}, u32[]{:S(2)}) %copy-start) | copy-done | bytes 2097176
  14.0 0.0 copy-start.3
  14.0 0.7 copy-done.3
  14.7 1.3 %shard_map.42 = (bf16[272,1024]{1,0:T(8,128)(2,1)}, bf16[272,1024]{1,0:T(8,128)(2,1)}) custom-call(bf16[1024,1024]{1,0:T(8,128)(2,1)S(1)} %copy-done, bf16[256,1024]{1,0:T(8,128)(2,1)S(1)} %slice.3._, s32[1,1024]{1,0:T(1,128)S(1)} %bitcast.4), custom_call_target="tpu_custom_call" | custom-call | flops 1024 | bytes 1024 | tf_op jit(solution)/shard_map/pallas_call | solution.py:287
  16.0 0.0 copy-start.4
  16.1 0.1 collective-permute-start.2
  16.2 0.0 copy-start.1
  16.2 3.5 %collective-permute-start.3 = (bf16[272,1024]{1,0:T(8,128)(2,1)}, bf16[272,1024]{1,0:T(8,128)(2,1)}, u32[]{:S(2)}, u32[]{:S(2)}) collective-permute-start(bf16[272,1024]{1,0:T(8,128)(2,1)} %get-tuple-element.30), channel_id=1, source_target_pairs={{1,2},{3,4},{5,6},{7,8},{9,10},{11,12},{13,14},{15,16},{17,18},{19... | collective-permute-start | bytes 1671176 | tf_op jit(solution)/shard_map/ppermute | solution.py:28
  19.6 0.0 collective-permute-done.refs_0_._
  19.6 5.3 %collective-permute-done.1.refs_1_.__ = bf16[256,1024]{1,0:T(8,128)(2,1)S(1)} collective-permute-done((bf16[256,1024]{1,0:T(8,128)(2,1)S(1)}, bf16[256,1024]{1,0:T(8,128)(2,1)S(1)}, u32[]{:S(2)}, u32[]{:S(2)}) %collective-permute-start.1) | collective-permute-done | bytes 524320 | tf_op jit(solution)/shard_map/ppermute | solution.py:28
  24.9 0.9 %shard_map.44 = bf16[384,1024]{1,0:T(8,128)(2,1)} custom-call(bf16[1024,1024]{1,0:T(8,128)(2,1)S(1)} %copy-done, bf16[256,1024]{1,0:T(8,128)(2,1)S(1)} %collective-permute-done.refs_0_._, bf16[256,1024]{1,0:T(8,128)(2,1)S(1)} %collective-permute-done.1.refs_1_.__), custom_call_target="tpu_custom_call" | custom-call | flops 1024 | bytes 1024 | tf_op jit(solution)/shard_map/pallas_call | solution.py:287
  25.9 0.1 collective-permute-start.6
  26.0 7.9 %collective-permute-start.7 = (bf16[384,1024]{1,0:T(8,128)(2,1)}, bf16[384,1024]{1,0:T(8,128)(2,1)}, u32[]{:S(2)}, u32[]{:S(2)}) collective-permute-start(bf16[384,1024]{1,0:T(8,128)(2,1)} %shard_map.44), channel_id=1, source_target_pairs={{1,2},{3,4},{5,6},{7,8},{9,10},{11,12},{13,14},{15,16},{17,18},{19... | collective-permute-start | bytes 2359304 | tf_op jit(solution)/shard_map/ppermute | solution.py:28
  33.8 0.0 copy-done.4
  33.8 1.0 %copy.4.row_ids_ref = s32[1024,1]{1,0:T(8,128)} copy(s32[1024,1]{0,1:T(1,128)S(1)} %bitcast.5) | data formatting | bytes 8192 | tf_op jit(solution)/shard_map/reshape | solution.py:330
  34.9 0.0 copy-done.1
  34.9 0.0 copy-start.2
  34.9 1.0 %copy-done.2 = s32[1024,1]{1,0:T(8,128)S(1)} copy-done((s32[1024,1]{1,0:T(8,128)S(1)}, s32[1024,1]{1,0:T(8,128)}, u32[]{:S(2)}) %copy-start.2) | copy-done | bytes 4120
  35.9 3.0 %shard_map.41 = (bf16[1024,1024]{1,0:T(8,128)(2,1)S(1)}, f32[1,1024]{1,0:T(1,128)S(1)}, f32[1,1024]{1,0:T(1,128)S(1)}) custom-call(bf16[1024,1024]{1,0:T(8,128)(2,1)S(1)} %copy-done.1, s32[1024,1]{1,0:T(8,128)S(1)} %copy-done.2, s32[1,1024]{1,0:T(1,128)S(1)} %bitcast.6), custom_call_target="tpu_custom_call" | custom-call | flops 1024 | bytes 1024 | tf_op jit(solution)/shard_map/pallas_call | solution.py:287
  38.9 0.0 collective-permute-done.2.refs_2_
  38.9 0.9 %collective-permute-done.3.refs_3_ = bf16[272,1024]{1,0:T(8,128)(2,1)} collective-permute-done((bf16[272,1024]{1,0:T(8,128)(2,1)}, bf16[272,1024]{1,0:T(8,128)(2,1)}, u32[]{:S(2)}, u32[]{:S(2)}) %collective-permute-start.3) | collective-permute-done | bytes 557088 | tf_op jit(solution)/shard_map/ppermute | solution.py:28
  39.8 4.6 %shard_map.43 = (bf16[256,1024]{1,0:T(8,128)(2,1)S(1)}, bf16[128,1024]{1,0:T(8,128)(2,1)S(1)}, bf16[128,1024]{1,0:T(8,128)(2,1)S(1)}, bf16[256,1024]{1,0:T(8,128...) custom-call(bf16[1024,1024]{1,0:T(8,128)(2,1)S(1)} %copy-done.1, ...), custom_call_target="tpu_custom_call" | custom-call | flops 1024 | bytes 1024 | tf_op jit(solution)/shard_map/pallas_call | solution.py:287
  44.4 0.1 collective-permute-start.4
  44.5 5.0 %collective-permute-start.5 = (bf16[128,1024]{1,0:T(8,128)(2,1)S(1)}, bf16[128,1024]{1,0:T(8,128)(2,1)S(1)}, u32[]{:S(2)}, u32[]{:S(2)}) collective-permute-start(bf16[128,1024]{1,0:T(8,128)(2,1)S(1)} %get-tuple-element.33), channel_id=1, source_target_pairs={{1,2},{3,4},{5,6},{7,8},{9,10},{11,12},{13,14},{15,16},{17,18},{19... | collective-permute-start | bytes 786440 | tf_op jit(solution)/shard_map/ppermute | solution.py:28
  49.6 0.0 collective-permute-done.6.side_0
  49.6 7.1 %collective-permute-done.7.side_1 = bf16[384,1024]{1,0:T(8,128)(2,1)} collective-permute-done((bf16[384,1024]{1,0:T(8,128)(2,1)}, bf16[384,1024]{1,0:T(8,128)(2,1)}, u32[]{:S(2)}, u32[]{:S(2)}) %collective-permute-start.7) | collective-permute-done | bytes 786464 | tf_op jit(solution)/shard_map/ppermute | solution.py:28
  56.6 4.4 %shard_map.45 = (bf16[384,1024]{1,0:T(8,128)(2,1)S(1)}, bf16[384,1024]{1,0:T(8,128)(2,1)S(1)}, f32[2,1024]{1,0:T(2,128)S(1)}, f32[2,1024]{1,0:T(2,128)S(1)}) custom-call(bf16[384,1024]{1,0:T(8,128)(2,1)} %collective-permute-done.6.side_0, bf16[384,1024]{1,0:T(8,128)(2,1)} %collective-permute-done.7.side_1, ...), custom_call_target="tpu_custom_call" | custom-call | flops 1024 | bytes 1024 | tf_op jit(solution)/shard_map/pallas_call | solution.py:287
  61.1 0.0 collective-permute-done.4.side_0
  61.1 0.0 collective-permute-done.5.side_1
  61.1 0.2 shard_map.46
  61.4 0.1 collective-permute-start.8
  61.5 6.1 %collective-permute-start.9 = (f32[2,1024]{1,0:T(2,128)S(1)}, f32[2,1024]{1,0:T(2,128)S(1)}, u32[]{:S(2)}, u32[]{:S(2)}) collective-permute-start(f32[2,1024]{1,0:T(2,128)S(1)} %get-tuple-element.49), channel_id=1, source_target_pairs={{1,2},{3,4},{5,6},{7,8},{9,10},{11,12},{13,14},{15,16},{17,18},{19... | collective-permute-start | bytes 24584 | tf_op jit(solution)/shard_map/ppermute | solution.py:28
  67.5 0.8 %shard_map.47.peaks = f32[2,1024]{1,0:T(2,128)S(1)} custom-call(bf16[128,1024]{1,0:T(8,128)(2,1)S(1)} %get-tuple-element.46.before, bf16[128,1024]{1,0:T(8,128)(2,1)S(1)} %get-tuple-element.47.after, bf16[1024,1024]{1,0:T(8,128)(2,1)S(1)} %get-tuple-element.31.refs_4_.normed, s32[8,1024]{1,0:T(8,128)S(1)} %get-tuple-element.34.bounds, ...), custom_call_target="tpu_custom_call" | custom-call | flops 1024 | bytes 1024 | tf_op jit(solution)/shard_map/pallas_call | solution.py:287
  68.3 0.0 collective-permute-done.8.side_0
  68.3 2.3 %collective-permute-done.9.side_1 = f32[2,1024]{1,0:T(2,128)S(1)} collective-permute-done((f32[2,1024]{1,0:T(2,128)S(1)}, f32[2,1024]{1,0:T(2,128)S(1)}, u32[]{:S(2)}, u32[]{:S(2)}) %collective-permute-start.9) | collective-permute-done | bytes 8224 | tf_op jit(solution)/shard_map/ppermute | solution.py:28
  70.6 0.6 shard_map.48
Async XLA Ops:
  1.7 17.9 %collective-permute-start = (bf16[256,1024]{1,0:T(8,128)(2,1)S(1)}, bf16[256,1024]{1,0:T(8,128)(2,1)S(1)}, u32[]{:S(2)}, u32[]{:S(2)}) collective-permute-start(bf16[256,1024]{1,0:T(8,128)(2,1)S(1)} %slice.3._), channel_id=1, source_target_pairs={{0,1},{2,3},{4,5},{6,7},{8,9},{10,11},{12,13},{14,15},{16,17},{18,... | collective-permute-start | bytes 1572872 | tf_op jit(solution)/shard_map/ppermute | solution.py:28
  3.7 21.2 %collective-permute-start.1 = (bf16[256,1024]{1,0:T(8,128)(2,1)S(1)}, bf16[256,1024]{1,0:T(8,128)(2,1)S(1)}, u32[]{:S(2)}, u32[]{:S(2)}) collective-permute-start(bf16[256,1024]{1,0:T(8,128)(2,1)S(1)} %slice.3._), channel_id=1, source_target_pairs={{1,2},{3,4},{5,6},{7,8},{9,10},{11,12},{13,14},{15,16},{17,18},{19... | collective-permute-start | bytes 1572872 | tf_op jit(solution)/shard_map/ppermute | solution.py:28
  12.4 1.6 %copy-start = (bf16[1024,1024]{1,0:T(8,128)(2,1)S(1)}, bf16[1024,1024]{1,0:T(8,128)(2,1)}, u32[]{:S(2)}) copy-start(bf16[1024,1024]{1,0:T(8,128)(2,1)} %raw_hbm.5) | copy-start | bytes 6291460
  14.0 0.7 copy-start.3
  16.0 17.8 %copy-start.4 = (s32[1024]{0:T(1024)S(1)}, s32[1024]{0:T(1024)}, u32[]{:S(2)}) copy-start(s32[1024]{0:T(1024)} %param.3) | copy-start | bytes 12292
  16.1 22.9 %collective-permute-start.2 = (bf16[272,1024]{1,0:T(8,128)(2,1)}, bf16[272,1024]{1,0:T(8,128)(2,1)}, u32[]{:S(2)}, u32[]{:S(2)}) collective-permute-start(bf16[272,1024]{1,0:T(8,128)(2,1)} %get-tuple-element.29), channel_id=1, source_target_pairs={{0,1},{2,3},{4,5},{6,7},{8,9},{10,11},{12,13},{14,15},{16,17},{18,... | collective-permute-start | bytes 1671176 | tf_op jit(solution)/shard_map/ppermute | solution.py:28
  16.2 18.7 %copy-start.1 = (bf16[1024,1024]{1,0:T(8,128)(2,1)S(1)}, bf16[1024,1024]{1,0:T(8,128)(2,1)}, u32[]{:S(2)}) copy-start(bf16[1024,1024]{1,0:T(8,128)(2,1)} %raw_hbm.5) | copy-start | bytes 6291460
  16.2 23.6 %collective-permute-start.3 = (bf16[272,1024]{1,0:T(8,128)(2,1)}, bf16[272,1024]{1,0:T(8,128)(2,1)}, u32[]{:S(2)}, u32[]{:S(2)}) collective-permute-start(bf16[272,1024]{1,0:T(8,128)(2,1)} %get-tuple-element.30), channel_id=1, source_target_pairs={{1,2},{3,4},{5,6},{7,8},{9,10},{11,12},{13,14},{15,16},{17,18},{19... | collective-permute-start | bytes 1671176 | tf_op jit(solution)/shard_map/ppermute | solution.py:28
  25.9 23.7 %collective-permute-start.6 = (bf16[384,1024]{1,0:T(8,128)(2,1)}, bf16[384,1024]{1,0:T(8,128)(2,1)}, u32[]{:S(2)}, u32[]{:S(2)}) collective-permute-start(bf16[384,1024]{1,0:T(8,128)(2,1)} %shard_map.44), channel_id=1, source_target_pairs={{0,1},{2,3},{4,5},{6,7},{8,9},{10,11},{12,13},{14,15},{16,17},{18,... | collective-permute-start | bytes 2359304 | tf_op jit(solution)/shard_map/ppermute | solution.py:28
  26.0 30.7 %collective-permute-start.7 = (bf16[384,1024]{1,0:T(8,128)(2,1)}, bf16[384,1024]{1,0:T(8,128)(2,1)}, u32[]{:S(2)}, u32[]{:S(2)}) collective-permute-start(bf16[384,1024]{1,0:T(8,128)(2,1)} %shard_map.44), channel_id=1, source_target_pairs={{1,2},{3,4},{5,6},{7,8},{9,10},{11,12},{13,14},{15,16},{17,18},{19... | collective-permute-start | bytes 2359304 | tf_op jit(solution)/shard_map/ppermute | solution.py:28
  34.9 1.0 %copy-start.2 = (s32[1024,1]{1,0:T(8,128)S(1)}, s32[1024,1]{1,0:T(8,128)}, u32[]{:S(2)}) copy-start(s32[1024,1]{1,0:T(8,128)} %copy.4.row_ids_ref) | copy-start | bytes 12292
  44.4 16.6 %collective-permute-start.4 = (bf16[128,1024]{1,0:T(8,128)(2,1)S(1)}, bf16[128,1024]{1,0:T(8,128)(2,1)S(1)}, u32[]{:S(2)}, u32[]{:S(2)}) collective-permute-start(bf16[128,1024]{1,0:T(8,128)(2,1)S(1)} %get-tuple-element.32), channel_id=1, source_target_pairs={{0,1},{2,3},{4,5},{6,7},{8,9},{10,11},{12,13},{14,15},{16,17},{18,... | collective-permute-start | bytes 786440 | tf_op jit(solution)/shard_map/ppermute | solution.py:28
  44.5 16.6 %collective-permute-start.5 = (bf16[128,1024]{1,0:T(8,128)(2,1)S(1)}, bf16[128,1024]{1,0:T(8,128)(2,1)S(1)}, u32[]{:S(2)}, u32[]{:S(2)}) collective-permute-start(bf16[128,1024]{1,0:T(8,128)(2,1)S(1)} %get-tuple-element.33), channel_id=1, source_target_pairs={{1,2},{3,4},{5,6},{7,8},{9,10},{11,12},{13,14},{15,16},{17,18},{19... | collective-permute-start | bytes 786440 | tf_op jit(solution)/shard_map/ppermute | solution.py:28
  61.4 7.0 %collective-permute-start.8 = (f32[2,1024]{1,0:T(2,128)S(1)}, f32[2,1024]{1,0:T(2,128)S(1)}, u32[]{:S(2)}, u32[]{:S(2)}) collective-permute-start(f32[2,1024]{1,0:T(2,128)S(1)} %get-tuple-element.49), channel_id=1, source_target_pairs={{0,1},{2,3},{4,5},{6,7},{8,9},{10,11},{12,13},{14,15},{16,17},{18,... | collective-permute-start | bytes 24584 | tf_op jit(solution)/shard_map/ppermute | solution.py:28
  61.5 9.2 %collective-permute-start.9 = (f32[2,1024]{1,0:T(2,128)S(1)}, f32[2,1024]{1,0:T(2,128)S(1)}, u32[]{:S(2)}, u32[]{:S(2)}) collective-permute-start(f32[2,1024]{1,0:T(2,128)S(1)} %get-tuple-element.49), channel_id=1, source_target_pairs={{1,2},{3,4},{5,6},{7,8},{9,10},{11,12},{13,14},{15,16},{17,18},{19... | collective-permute-start | bytes 24584 | tf_op jit(solution)/shard_map/ppermute | solution.py:28

commit v4 on v3

--- a/solution.py
+++ b/solution.py
@@ -251,7 +251,7 @@
 
 def next_kernel(chunk, side_0, side_1, normed, bounds, peaks_in, returned_in, *refs):
     befores, afters = refs[:chunk], refs[chunk : 2 * chunk]
-    before, after, peaks, returned = refs[2 * chunk :]
+    peaks, returned, before, after = refs[2 * chunk :]
     peaks[...] = peaks_in[...]
     returned[...] = returned_in[...]
     take_chunk(side_0, side_1, before, after)
@@ -259,12 +259,12 @@
     across(chunk, [*befores, before], [*afters, after], bounds, returned)
 
 
-def last_across_kernel(chunk, side_0, side_1, bounds, returned_in, *refs):
-    befores, afters = refs[:chunk], refs[chunk : 2 * chunk]
-    before, after, returned = refs[2 * chunk :]
+def last_across_kernel(side_0, side_1, edge_before, edge_after, bounds, returned_in, *refs):
+    before, after, returned = refs
     returned[...] = returned_in[...]
     take_chunk(side_0, side_1, before, after)
-    across(chunk, [*befores, before], [*afters, after], bounds, returned)
+    across_edges = [None, None, edge_before, None, before], [None, None, edge_after, None, after]
+    across(4, *across_edges, bounds, returned)
 
 
 def last_own_kernel(chunk, before, after, normed, bounds, peaks_in, peaks):
@@ -339,17 +339,16 @@
     )
     last = exchanged(cut_0, cut_1)
     befores, afters = new[:3], new[3:]
-    before, after, peaks, returned = call(
+    peaks, returned = call(
         functools.partial(next_kernel, 3),
-        [sizes[3], sizes[3], vectors(2), vectors(2)],
+        [vectors(2), vectors(2)],
         (*middle, normed, bounds, peaks, returned, *befores, *afters),
-    )
-    befores.append(before)
-    afters.append(after)
+        scratch=[pltpu.VMEM((SIZES[3], WIDTH), jnp.bfloat16)] * 2,
+    )
     before, after, returned = call(
-        functools.partial(last_across_kernel, 4),
+        last_across_kernel,
         [sizes[4], sizes[4], vectors(2)],
-        (*last, bounds, returned, *befores, *afters),
+        (*last, befores[2], afters[2], bounds, returned),
     )
     sent_back = exchanged(returned, returned)
     (peaks,) = call(

time: 71.8 us -> 71.6 us (level)
  waiting for transfers between devices: 15.5 us -> 14.6 us
  Pallas kernels: 15.9 us -> 16.7 us
    ppermute x10, waiting for transfers between devices: 15.5 us -> 14.6 us  [exchanged(): got.append(lax.ppermute(block, AXES, pairs + [(b, a) for a, b in pairs]))]
    pallas_call x8, Pallas kernels: 15.9 us -> 16.7 us  [call(): pl.pallas_call(kernel, out_shape=outs, in_specs=[pl.BlockSpec(memory_spac...]
  transfers between devices with their start and end apart: 10 -> 10, of which waited for: 4 -> 4; matrix products, arithmetic and copies ran while one was open for 1% -> 1% of each run, Pallas kernels for 21% -> 22%
where the time goes in v4:
time: 71.6 us; the launch traced here: 71.1 us
  starting transfers between devices  33.6 us (47%)
  Pallas kernels  16.7 us (23%)
  waiting for transfers between devices  14.6 us (20%)
  local copies, waits for them, and re-layouts  5.44 us (8%)
  between operations  0.84 us (1%)
    ppermute x10, starting transfers between devices, exchanged(): got.append(lax.ppermute(block, AXES, pairs + [(b, a) for a, b in pairs]))  33.6 us
    pallas_call x8, Pallas kernels, call(): pl.pallas_call(kernel, out_shape=outs, in_specs=[pl.BlockSpec(memory_spac...  16.7 us
    ppermute x10, waiting for transfers between devices, exchanged(): got.append(lax.ppermute(block, AXES, pairs + [(b, a) for a, b in pairs]))  14.6 us
    unnamed x10, local copies, waits for them, and re-layouts  3.33 us
  transfers between devices with their start and end apart: 10, of which 4 were waited for; matrix products, arithmetic and copies ran while one was open for 1% of the time, Pallas kernels for 22%

profile of v4, /device:TPU:6, one launch (start us, length us, event | category | flops | bytes accessed | tf_op | source)
XLA Modules:
  0.0 71.1 jit_solution(14062867196747507565)
XLA Ops:
  0.6 1.1 %slice.3._ = bf16[256,1024]{1,0:T(8,128)(2,1)S(1)} slice(bf16[1024,1024]{1,0:T(8,128)(2,1)} %raw_hbm.5), slice={[256:512], [0:1024]} | slice | bytes 1048576 | tf_op jit(solution)/shard_map/slice | solution.py:309
  1.7 2.0 %collective-permute-start = (bf16[256,1024]{1,0:T(8,128)(2,1)S(1)}, bf16[256,1024]{1,0:T(8,128)(2,1)S(1)}, u32[]{:S(2)}, u32[]{:S(2)}) collective-permute-start(bf16[256,1024]{1,0:T(8,128)(2,1)S(1)} %slice.3._), channel_id=1, source_target_pairs={{0,1},{2,3},{4,5},{6,7},{8,9},{10,11},{12,13},{14,15},{16,17},{18,... | collective-permute-start | bytes 1572872 | tf_op jit(solution)/shard_map/ppermute | solution.py:28
  3.7 8.7 %collective-permute-start.1 = (bf16[256,1024]{1,0:T(8,128)(2,1)S(1)}, bf16[256,1024]{1,0:T(8,128)(2,1)S(1)}, u32[]{:S(2)}, u32[]{:S(2)}) collective-permute-start(bf16[256,1024]{1,0:T(8,128)(2,1)S(1)} %slice.3._), channel_id=1, source_target_pairs={{1,2},{3,4},{5,6},{7,8},{9,10},{11,12},{13,14},{15,16},{17,18},{19... | collective-permute-start | bytes 1572872 | tf_op jit(solution)/shard_map/ppermute | solution.py:28
  12.4 0.0 copy-start
  12.5 1.6 %copy-done = bf16[1024,1024]{1,0:T(8,128)(2,1)S(1)} copy-done((bf16[1024,1024]{1,0:T(8,128)(2,1)S(1)}, bf16[1024,1024]{1,0:T(8,128)(2,1)}, u32[]{:S(2)}) %copy-start) | copy-done | bytes 2097176
  14.0 0.0 copy-start.3
  14.0 0.7 copy-done.3
  14.7 1.3 %shard_map.42 = (bf16[272,1024]{1,0:T(8,128)(2,1)}, bf16[272,1024]{1,0:T(8,128)(2,1)}) custom-call(bf16[1024,1024]{1,0:T(8,128)(2,1)S(1)} %copy-done, bf16[256,1024]{1,0:T(8,128)(2,1)S(1)} %slice.3._, s32[1,1024]{1,0:T(1,128)S(1)} %bitcast.4), custom_call_target="tpu_custom_call" | custom-call | flops 1024 | bytes 1024 | tf_op jit(solution)/shard_map/pallas_call | solution.py:287
  16.0 0.0 copy-start.4
  16.1 0.1 collective-permute-start.2
  16.2 0.0 copy-start.1
  16.2 3.5 %collective-permute-start.3 = (bf16[272,1024]{1,0:T(8,128)(2,1)}, bf16[272,1024]{1,0:T(8,128)(2,1)}, u32[]{:S(2)}, u32[]{:S(2)}) collective-permute-start(bf16[272,1024]{1,0:T(8,128)(2,1)} %get-tuple-element.28), channel_id=1, source_target_pairs={{1,2},{3,4},{5,6},{7,8},{9,10},{11,12},{13,14},{15,16},{17,18},{19... | collective-permute-start | bytes 1671176 | tf_op jit(solution)/shard_map/ppermute | solution.py:28
  19.6 0.0 collective-permute-done.refs_0_._
  19.6 5.3 %collective-permute-done.1.refs_1_.__ = bf16[256,1024]{1,0:T(8,128)(2,1)S(1)} collective-permute-done((bf16[256,1024]{1,0:T(8,128)(2,1)S(1)}, bf16[256,1024]{1,0:T(8,128)(2,1)S(1)}, u32[]{:S(2)}, u32[]{:S(2)}) %collective-permute-start.1) | collective-permute-done | bytes 524320 | tf_op jit(solution)/shard_map/ppermute | solution.py:28
  24.9 0.9 %shard_map.44 = bf16[384,1024]{1,0:T(8,128)(2,1)} custom-call(bf16[1024,1024]{1,0:T(8,128)(2,1)S(1)} %copy-done, bf16[256,1024]{1,0:T(8,128)(2,1)S(1)} %collective-permute-done.refs_0_._, bf16[256,1024]{1,0:T(8,128)(2,1)S(1)} %collective-permute-done.1.refs_1_.__), custom_call_target="tpu_custom_call" | custom-call | flops 1024 | bytes 1024 | tf_op jit(solution)/shard_map/pallas_call | solution.py:287
  25.9 0.1 collective-permute-start.6
  26.0 7.9 %collective-permute-start.7 = (bf16[384,1024]{1,0:T(8,128)(2,1)}, bf16[384,1024]{1,0:T(8,128)(2,1)}, u32[]{:S(2)}, u32[]{:S(2)}) collective-permute-start(bf16[384,1024]{1,0:T(8,128)(2,1)} %shard_map.44), channel_id=1, source_target_pairs={{1,2},{3,4},{5,6},{7,8},{9,10},{11,12},{13,14},{15,16},{17,18},{19... | collective-permute-start | bytes 2359304 | tf_op jit(solution)/shard_map/ppermute | solution.py:28
  33.8 0.0 copy-done.4
  33.8 1.0 %copy.4.row_ids_ref = s32[1024,1]{1,0:T(8,128)} copy(s32[1024,1]{0,1:T(1,128)S(1)} %bitcast.5) | data formatting | bytes 8192 | tf_op jit(solution)/shard_map/reshape | solution.py:330
  34.9 0.0 copy-done.1
  34.9 0.0 copy-start.2
  34.9 1.0 %copy-done.2 = s32[1024,1]{1,0:T(8,128)S(1)} copy-done((s32[1024,1]{1,0:T(8,128)S(1)}, s32[1024,1]{1,0:T(8,128)}, u32[]{:S(2)}) %copy-start.2) | copy-done | bytes 4120
  35.9 3.0 %shard_map.41 = (bf16[1024,1024]{1,0:T(8,128)(2,1)S(1)}, f32[1,1024]{1,0:T(1,128)S(1)}, f32[1,1024]{1,0:T(1,128)S(1)}) custom-call(bf16[1024,1024]{1,0:T(8,128)(2,1)S(1)} %copy-done.1, s32[1024,1]{1,0:T(8,128)S(1)} %copy-done.2, s32[1,1024]{1,0:T(1,128)S(1)} %bitcast.6), custom_call_target="tpu_custom_call" | custom-call | flops 1024 | bytes 1024 | tf_op jit(solution)/shard_map/pallas_call | solution.py:287
  38.9 0.0 collective-permute-done.2.refs_2_
  38.9 0.9 %collective-permute-done.3.refs_3_ = bf16[272,1024]{1,0:T(8,128)(2,1)} collective-permute-done((bf16[272,1024]{1,0:T(8,128)(2,1)}, bf16[272,1024]{1,0:T(8,128)(2,1)}, u32[]{:S(2)}, u32[]{:S(2)}) %collective-permute-start.3) | collective-permute-done | bytes 557088 | tf_op jit(solution)/shard_map/ppermute | solution.py:28
  39.8 5.4 %shard_map.43 = (bf16[256,1024]{1,0:T(8,128)(2,1)S(1)}, bf16[128,1024]{1,0:T(8,128)(2,1)S(1)}, bf16[128,1024]{1,0:T(8,128)(2,1)S(1)}, bf16[256,1024]{1,0:T(8,128...) custom-call(bf16[1024,1024]{1,0:T(8,128)(2,1)S(1)} %copy-done.1, ...), custom_call_target="tpu_custom_call" | custom-call | flops 1024 | bytes 1024 | tf_op jit(solution)/shard_map/pallas_call | solution.py:287
  45.2 0.1 collective-permute-start.4
  45.3 5.0 %collective-permute-start.5 = (bf16[128,1024]{1,0:T(8,128)(2,1)S(1)}, bf16[128,1024]{1,0:T(8,128)(2,1)S(1)}, u32[]{:S(2)}, u32[]{:S(2)}) collective-permute-start(bf16[128,1024]{1,0:T(8,128)(2,1)S(1)} %get-tuple-element.31), channel_id=1, source_target_pairs={{1,2},{3,4},{5,6},{7,8},{9,10},{11,12},{13,14},{15,16},{17,18},{19... | collective-permute-start | bytes 786440 | tf_op jit(solution)/shard_map/ppermute | solution.py:28
  50.3 0.0 collective-permute-done.6.side_0
  50.3 6.2 %collective-permute-done.7.side_1 = bf16[384,1024]{1,0:T(8,128)(2,1)} collective-permute-done((bf16[384,1024]{1,0:T(8,128)(2,1)}, bf16[384,1024]{1,0:T(8,128)(2,1)}, u32[]{:S(2)}, u32[]{:S(2)}) %collective-permute-start.7) | collective-permute-done | bytes 786464 | tf_op jit(solution)/shard_map/ppermute | solution.py:28
  56.5 4.4 %shard_map.45 = (f32[2,1024]{1,0:T(2,128)S(1)}, f32[2,1024]{1,0:T(2,128)S(1)}) custom-call(bf16[384,1024]{1,0:T(8,128)(2,1)} %collective-permute-done.6.side_0, bf16[384,1024]{1,0:T(8,128)(2,1)} %collective-permute-done.7.side_1, bf16[1024,1024]{1,0:T(8,128)(2,1)S(1)} %get-tuple-element.29.refs_4_.normed, s32[8,1024]{1,0:T(8,128)S(1)} %get-tuple-element.34.bounds, ...), custom_call_target="tpu_custom_call" | custom-call | flops 1024 | bytes 1024 | tf_op jit(solution)/shard_map/pallas_call | solution.py:287
  61.0 0.0 collective-permute-done.4.side_0
  61.0 0.0 collective-permute-done.5.side_1
  61.0 0.2 shard_map.46
  61.2 0.1 collective-permute-start.8
  61.3 6.2 %collective-permute-start.9 = (f32[2,1024]{1,0:T(2,128)S(1)}, f32[2,1024]{1,0:T(2,128)S(1)}, u32[]{:S(2)}, u32[]{:S(2)}) collective-permute-start(f32[2,1024]{1,0:T(2,128)S(1)} %get-tuple-element.45), channel_id=1, source_target_pairs={{1,2},{3,4},{5,6},{7,8},{9,10},{11,12},{13,14},{15,16},{17,18},{19... | collective-permute-start | bytes 24584 | tf_op jit(solution)/shard_map/ppermute | solution.py:28
  67.5 0.8 %shard_map.47.peaks = f32[2,1024]{1,0:T(2,128)S(1)} custom-call(bf16[128,1024]{1,0:T(8,128)(2,1)S(1)} %get-tuple-element.42.before, bf16[128,1024]{1,0:T(8,128)(2,1)S(1)} %get-tuple-element.43.after, bf16[1024,1024]{1,0:T(8,128)(2,1)S(1)} %get-tuple-element.29.refs_4_.normed, s32[8,1024]{1,0:T(8,128)S(1)} %get-tuple-element.34.bounds, ...), custom_call_target="tpu_custom_call" | custom-call | flops 1024 | bytes 1024 | tf_op jit(solution)/shard_map/pallas_call | solution.py:287
  68.3 0.0 collective-permute-done.8.side_0
  68.3 2.2 %collective-permute-done.9.side_1 = f32[2,1024]{1,0:T(2,128)S(1)} collective-permute-done((f32[2,1024]{1,0:T(2,128)S(1)}, f32[2,1024]{1,0:T(2,128)S(1)}, u32[]{:S(2)}, u32[]{:S(2)}) %collective-permute-start.9) | collective-permute-done | bytes 8224 | tf_op jit(solution)/shard_map/ppermute | solution.py:28
  70.5 0.6 shard_map.48
Async XLA Ops:
  1.7 17.9 %collective-permute-start = (bf16[256,1024]{1,0:T(8,128)(2,1)S(1)}, bf16[256,1024]{1,0:T(8,128)(2,1)S(1)}, u32[]{:S(2)}, u32[]{:S(2)}) collective-permute-start(bf16[256,1024]{1,0:T(8,128)(2,1)S(1)} %slice.3._), channel_id=1, source_target_pairs={{0,1},{2,3},{4,5},{6,7},{8,9},{10,11},{12,13},{14,15},{16,17},{18,... | collective-permute-start | bytes 1572872 | tf_op jit(solution)/shard_map/ppermute | solution.py:28
  3.7 21.2 %collective-permute-start.1 = (bf16[256,1024]{1,0:T(8,128)(2,1)S(1)}, bf16[256,1024]{1,0:T(8,128)(2,1)S(1)}, u32[]{:S(2)}, u32[]{:S(2)}) collective-permute-start(bf16[256,1024]{1,0:T(8,128)(2,1)S(1)} %slice.3._), channel_id=1, source_target_pairs={{1,2},{3,4},{5,6},{7,8},{9,10},{11,12},{13,14},{15,16},{17,18},{19... | collective-permute-start | bytes 1572872 | tf_op jit(solution)/shard_map/ppermute | solution.py:28
  12.4 1.6 %copy-start = (bf16[1024,1024]{1,0:T(8,128)(2,1)S(1)}, bf16[1024,1024]{1,0:T(8,128)(2,1)}, u32[]{:S(2)}) copy-start(bf16[1024,1024]{1,0:T(8,128)(2,1)} %raw_hbm.5) | copy-start | bytes 6291460
  14.0 0.7 copy-start.3
  16.0 17.8 %copy-start.4 = (s32[1024]{0:T(1024)S(1)}, s32[1024]{0:T(1024)}, u32[]{:S(2)}) copy-start(s32[1024]{0:T(1024)} %param.3) | copy-start | bytes 12292
  16.1 22.9 %collective-permute-start.2 = (bf16[272,1024]{1,0:T(8,128)(2,1)}, bf16[272,1024]{1,0:T(8,128)(2,1)}, u32[]{:S(2)}, u32[]{:S(2)}) collective-permute-start(bf16[272,1024]{1,0:T(8,128)(2,1)} %get-tuple-element.27), channel_id=1, source_target_pairs={{0,1},{2,3},{4,5},{6,7},{8,9},{10,11},{12,13},{14,15},{16,17},{18,... | collective-permute-start | bytes 1671176 | tf_op jit(solution)/shard_map/ppermute | solution.py:28
  16.2 18.7 %copy-start.1 = (bf16[1024,1024]{1,0:T(8,128)(2,1)S(1)}, bf16[1024,1024]{1,0:T(8,128)(2,1)}, u32[]{:S(2)}) copy-start(bf16[1024,1024]{1,0:T(8,128)(2,1)} %raw_hbm.5) | copy-start | bytes 6291460
  16.2 23.6 %collective-permute-start.3 = (bf16[272,1024]{1,0:T(8,128)(2,1)}, bf16[272,1024]{1,0:T(8,128)(2,1)}, u32[]{:S(2)}, u32[]{:S(2)}) collective-permute-start(bf16[272,1024]{1,0:T(8,128)(2,1)} %get-tuple-element.28), channel_id=1, source_target_pairs={{1,2},{3,4},{5,6},{7,8},{9,10},{11,12},{13,14},{15,16},{17,18},{19... | collective-permute-start | bytes 1671176 | tf_op jit(solution)/shard_map/ppermute | solution.py:28
  25.9 24.5 %collective-permute-start.6 = (bf16[384,1024]{1,0:T(8,128)(2,1)}, bf16[384,1024]{1,0:T(8,128)(2,1)}, u32[]{:S(2)}, u32[]{:S(2)}) collective-permute-start(bf16[384,1024]{1,0:T(8,128)(2,1)} %shard_map.44), channel_id=1, source_target_pairs={{0,1},{2,3},{4,5},{6,7},{8,9},{10,11},{12,13},{14,15},{16,17},{18,... | collective-permute-start | bytes 2359304 | tf_op jit(solution)/shard_map/ppermute | solution.py:28
  26.0 30.6 %collective-permute-start.7 = (bf16[384,1024]{1,0:T(8,128)(2,1)}, bf16[384,1024]{1,0:T(8,128)(2,1)}, u32[]{:S(2)}, u32[]{:S(2)}) collective-permute-start(bf16[384,1024]{1,0:T(8,128)(2,1)} %shard_map.44), channel_id=1, source_target_pairs={{1,2},{3,4},{5,6},{7,8},{9,10},{11,12},{13,14},{15,16},{17,18},{19... | collective-permute-start | bytes 2359304 | tf_op jit(solution)/shard_map/ppermute | solution.py:28
  34.9 1.0 %copy-start.2 = (s32[1024,1]{1,0:T(8,128)S(1)}, s32[1024,1]{1,0:T(8,128)}, u32[]{:S(2)}) copy-start(s32[1024,1]{1,0:T(8,128)} %copy.4.row_ids_ref) | copy-start | bytes 12292
  45.2 15.8 %collective-permute-start.4 = (bf16[128,1024]{1,0:T(8,128)(2,1)S(1)}, bf16[128,1024]{1,0:T(8,128)(2,1)S(1)}, u32[]{:S(2)}, u32[]{:S(2)}) collective-permute-start(bf16[128,1024]{1,0:T(8,128)(2,1)S(1)} %get-tuple-element.30), channel_id=1, source_target_pairs={{0,1},{2,3},{4,5},{6,7},{8,9},{10,11},{12,13},{14,15},{16,17},{18,... | collective-permute-start | bytes 786440 | tf_op jit(solution)/shard_map/ppermute | solution.py:28
  45.3 15.7 %collective-permute-start.5 = (bf16[128,1024]{1,0:T(8,128)(2,1)S(1)}, bf16[128,1024]{1,0:T(8,128)(2,1)S(1)}, u32[]{:S(2)}, u32[]{:S(2)}) collective-permute-start(bf16[128,1024]{1,0:T(8,128)(2,1)S(1)} %get-tuple-element.31), channel_id=1, source_target_pairs={{1,2},{3,4},{5,6},{7,8},{9,10},{11,12},{13,14},{15,16},{17,18},{19... | collective-permute-start | bytes 786440 | tf_op jit(solution)/shard_map/ppermute | solution.py:28
  61.2 7.1 %collective-permute-start.8 = (f32[2,1024]{1,0:T(2,128)S(1)}, f32[2,1024]{1,0:T(2,128)S(1)}, u32[]{:S(2)}, u32[]{:S(2)}) collective-permute-start(f32[2,1024]{1,0:T(2,128)S(1)} %get-tuple-element.45), channel_id=1, source_target_pairs={{0,1},{2,3},{4,5},{6,7},{8,9},{10,11},{12,13},{14,15},{16,17},{18,... | collective-permute-start | bytes 24584 | tf_op jit(solution)/shard_map/ppermute | solution.py:28
  61.3 9.2 %collective-permute-start.9 = (f32[2,1024]{1,0:T(2,128)S(1)}, f32[2,1024]{1,0:T(2,128)S(1)}, u32[]{:S(2)}, u32[]{:S(2)}) collective-permute-start(f32[2,1024]{1,0:T(2,128)S(1)} %get-tuple-element.45), channel_id=1, source_target_pairs={{1,2},{3,4},{5,6},{7,8},{9,10},{11,12},{13,14},{15,16},{17,18},{19... | collective-permute-start | bytes 24584 | tf_op jit(solution)/shard_map/ppermute | solution.py:28
